TPU v7x, 32 devices: a whole 2x2x4 slice. The times are simulated.
32 devices in a mesh: dp: 8 (over z, y), code: 4 (over x, core).
Axes of the slice: x: 2, y: 2, z: 4, core: 2. Of those that a mesh axis runs over, the one named last changes fastest.
Arguments:
- crops_in: bfloat16 [4, 16, 256, 512], P('code', None, 'dp'), may hold values from -6 to 6
- crop_weight: bfloat16 [4, 16], P('code', 'dp'), may hold values from 0.7 to 6
- cotangent: bfloat16 [4, 16, 64, 256], P('code', 'dp'), may hold values from -6 to 6
- conv_copy: bfloat16 [512, 2, 9, 512], replicated, may hold values from -0.09375 to 0.09375
- down_copy: bfloat16 [512, 4, 512], replicated, may hold values from -0.125 to 0.125
- proj_copy: bfloat16 [512, 256], replicated, may hold values from -0.25 to 0.25
- norm_copy: bfloat16 [512, 4], replicated, may hold values from -0.95 to 1.5
- codebook: bfloat16 [16384, 256], P('code'), may hold values from -5 to 5
- conv_master: float32 [512, 2, 9, 512], P('dp', None, None, 'code'), may hold values from -0.09375 to 0.09375
- conv_moment: float32 [512, 2, 9, 512], P('dp', None, None, 'code'), may hold values from -7680 to 7680
- conv_average: float32 [512, 2, 9, 512], P('dp', None, None, 'code'), may hold values from -0.09375 to 0.09375
- down_master: float32 [512, 4, 512], P('dp', None, 'code'), may hold values from -0.125 to 0.125
- down_moment: float32 [512, 4, 512], P('dp', None, 'code'), may hold values from -384 to 384
- down_average: float32 [512, 4, 512], P('dp', None, 'code'), may hold values from -0.125 to 0.125
- proj_master: float32 [512, 256], P('dp', 'code'), may hold values from -0.25 to 0.25
- proj_moment: float32 [512, 256], P('dp', 'code'), may hold values from -512 to 512
- proj_average: float32 [512, 256], P('dp', 'code'), may hold values from -0.25 to 0.25
- norm_master: float32 [512, 4], replicated, may hold values from 0.5 to 1.5
- norm_moment: float32 [512, 4], replicated, may hold values from -192 to 192
- norm_average: float32 [512, 4], replicated, may hold values from 0.5 to 1.5
- code_master: float32 [16384, 256], P('code', 'dp'), may hold values from -5 to 5
- code_moment: float32 [16384, 256], P('code', 'dp'), may hold values from -6 to 6
- code_average: float32 [16384, 256], P('code', 'dp'), may hold values from -5 to 5
- repl_code: int32 [4, 64], replicated, may hold values from 0 to 16383, as said below
- repl_src: int32 [4, 64], replicated, may hold values from 0 to 4095
Outputs:
- quantized: float32 [4, 16, 64, 256], P('code', 'dp')
- input_grad: float32 [4, 16, 256, 512], P('code', None, 'dp')
- conv_moment_new: float32 [512, 2, 9, 512], P('dp', None, None, 'code')
- conv_master_new: float32 [512, 2, 9, 512], P('dp', None, None, 'code')
- conv_average_new: float32 [512, 2, 9, 512], P('dp', None, None, 'code')
- down_moment_new: float32 [512, 4, 512], P('dp', None, 'code')
- down_master_new: float32 [512, 4, 512], P('dp', None, 'code')
- down_average_new: float32 [512, 4, 512], P('dp', None, 'code')
- proj_moment_new: float32 [512, 256], P('dp', 'code')
- proj_master_new: float32 [512, 256], P('dp', 'code')
- proj_average_new: float32 [512, 256], P('dp', 'code')
- norm_moment_new: float32 [512, 4], replicated
- norm_master_new: float32 [512, 4], replicated
- norm_average_new: float32 [512, 4], replicated
- code_moment_new: float32 [16384, 256], P('code', 'dp')
- code_master_new: float32 [16384, 256], P('code', 'dp')
- code_average_new: float32 [16384, 256], P('code', 'dp')
- code_load: float32 [16384], P('code')
Inputs may be any that keep to these rules, and one draw needn't show every extreme that they name: `repl_code`: the 4 x 64 codes are all different.
All inputs are finite; a program needn't handle non-finite values.
Results may differ from a plain program's by a relative error of at most 0.014.
Values may be sent and summed in bfloat16 or wider, within the bound.
No kernel may reach another device: no remote copies, remote signals or barrier semaphores. Data moves between devices by JAX's collectives and lax.ppermute only.
A program may use at most 256 MiB of HBM per device.

v0:
```python
import math

import jax
import jax.numpy as jnp
from jax import lax
from jax.sharding import PartitionSpec as P

GROUPS = 32
DEPTH = 4


BETA = 0.0625
EPSILON = 1e-05
MOMENTUM = 0.5
AVERAGE_DECAY = 0.5
COMMIT = 0.25
WEIGHT_RATE = 0.05
NORM_RATE = 0.5
CODE_RATE = 0.5
HIGH = lax.Precision.HIGHEST


def combined_all(array, axis, combine):
    everything = jax.tree.map(
        lambda part, kind: lax.all_gather(part.astype(kind), axis),
        array,
        (jnp.bfloat16, jnp.bfloat16, jnp.bfloat16),
    )

    def take(k):
        return jax.tree.map(lambda part, own: part[k].astype(own.dtype), everything, array)

    return lax.fori_loop(
        1, lax.axis_size(axis), lambda k, so_far: combine(so_far, take(k)), take(0)
    )


def group_norm(values, gain, bias):
    crops, pixels, channels = values.shape
    grouped = values.reshape(crops, pixels, GROUPS, channels // GROUPS)
    center = jnp.mean(grouped, axis=(1, 3), keepdims=True)
    shifted = grouped - center
    spread = jnp.mean(shifted * shifted, axis=(1, 3), keepdims=True)
    inverse = lax.rsqrt(spread + EPSILON)
    normed = (shifted * inverse).reshape(crops, pixels, channels)
    return (normed * gain + bias, normed, inverse)


def group_back(grad_out, normed, inverse, gain):
    crops, pixels, channels = grad_out.shape
    grad_gain = jnp.sum(grad_out * normed, axis=(0, 1))
    grad_bias = jnp.sum(grad_out, axis=(0, 1))
    grad_normed = (grad_out * gain).reshape(crops, pixels, GROUPS, channels // GROUPS)
    grouped = normed.reshape(crops, pixels, GROUPS, channels // GROUPS)
    first_mean = jnp.mean(grad_normed, axis=(1, 3), keepdims=True)
    second_mean = jnp.mean(grad_normed * grouped, axis=(1, 3), keepdims=True)
    grad_values = inverse * (grad_normed - first_mean - grouped * second_mean)
    return (grad_values.reshape(crops, pixels, channels), grad_gain, grad_bias)


def silu_slope(values):
    sigma = jax.nn.sigmoid(values)
    return sigma * (1.0 + values * (1.0 - sigma))


def conv_forward(image, weight, side):
    crops = image.shape[0]
    grid = image.reshape(crops, side, side, image.shape[2])
    padded = jnp.pad(grid, ((0, 0), (1, 1), (1, 1), (0, 0)))
    result = jnp.zeros((crops, side, side, weight.shape[2]), jnp.float32)
    for tap in range(9):
        window = padded[:, tap // 3 : tap // 3 + side, tap % 3 : tap % 3 + side, :]
        result = result + jnp.einsum(
            "bhwc,cd->bhwd", window, weight[:, tap, :], preferred_element_type=jnp.float32
        )
    return result.reshape(crops, side * side, weight.shape[2])


def conv_backward(image, grad_out, weight, side):
    crops, pixels, channels = image.shape
    grid = image.reshape(crops, side, side, channels)
    padded = jnp.pad(grid, ((0, 0), (1, 1), (1, 1), (0, 0)))
    grad_grid = grad_out.reshape(crops, side, side, grad_out.shape[2])
    grad_padded = jnp.pad(grad_grid, ((0, 0), (1, 1), (1, 1), (0, 0)))
    grad_image = jnp.zeros((crops, side, side, channels), jnp.float32)
    taps = []
    for tap in range(9):
        row_at = tap // 3
        col_at = tap % 3
        window = padded[:, row_at : row_at + side, col_at : col_at + side, :]
        taps.append(
            jnp.einsum("bhwc,bhwd->cd", window, grad_grid, preferred_element_type=jnp.float32)
        )
        back_window = grad_padded[
            :, 2 - row_at : 2 - row_at + side, 2 - col_at : 2 - col_at + side, :
        ]
        grad_image = grad_image + jnp.einsum(
            "bhwd,cd->bhwc", back_window, weight[:, tap, :], preferred_element_type=jnp.float32
        )
    return (grad_image.reshape(crops, pixels, channels), jnp.stack(taps, axis=1))


def down_forward(image, weight, side):
    crops = image.shape[0]
    half = side // 2
    grid = image.reshape(crops, side, side, image.shape[2])
    result = jnp.zeros((crops, half, half, weight.shape[2]), jnp.float32)
    for tap in range(4):
        window = grid[:, tap // 2 :: 2, tap % 2 :: 2, :]
        result = result + jnp.einsum(
            "bhwc,cd->bhwd", window, weight[:, tap, :], preferred_element_type=jnp.float32
        )
    return result.reshape(crops, half * half, weight.shape[2])


def down_backward(image, grad_out, weight, side):
    crops, pixels, channels = image.shape
    half = side // 2
    grid = image.reshape(crops, side, side, channels)
    grad_grid = grad_out.reshape(crops, half, half, grad_out.shape[2])
    taps = []
    pieces = []
    for tap in range(4):
        window = grid[:, tap // 2 :: 2, tap % 2 :: 2, :]
        taps.append(
            jnp.einsum("bhwc,bhwd->cd", window, grad_grid, preferred_element_type=jnp.float32)
        )
        pieces.append(
            jnp.einsum(
                "bhwd,cd->bhwc", grad_grid, weight[:, tap, :], preferred_element_type=jnp.float32
            )
        )
    stacked = jnp.stack(pieces, axis=0).reshape(2, 2, crops, half, half, channels)
    grad_image = stacked.transpose(2, 3, 0, 4, 1, 5).reshape(crops, pixels, channels)
    return (grad_image, jnp.stack(taps, axis=1))


def block_scores(rows_low, codes, norms):
    inner = jnp.einsum("re,ke->rk", rows_low, codes, preferred_element_type=jnp.float32)
    return BETA * (2.0 * inner - norms[None, :])


def soft_forward(rows_low, codes, norms):
    scores = block_scores(rows_low, codes, norms)
    peak = jnp.max(scores, axis=1)
    powers = jnp.exp(scores - peak[:, None])
    weighted = jnp.einsum(
        "rk,ke->re", powers.astype(jnp.bfloat16), codes, preferred_element_type=jnp.float32
    )
    return (peak, jnp.sum(powers, axis=1), weighted)


def combine_soft(first, second):
    peak = jnp.maximum(first[0], second[0])
    scale_first = jnp.exp(first[0] - peak)
    scale_second = jnp.exp(second[0] - peak)
    total = first[1] * scale_first + second[1] * scale_second
    weighted = first[2] * scale_first[:, None] + second[2] * scale_second[:, None]
    return (peak, total, weighted)


def soft_backward(
    rows_low, peak, scale, inverse_total, grad_picked, picked, weight, codes, codes_wide, norms
):
    scores = block_scores(rows_low, codes, norms)
    powers = jnp.exp(scores - peak[:, None])
    factor = scale * inverse_total
    grad_weighted = (grad_picked * factor[:, None]).astype(jnp.bfloat16)
    grad_total = -jnp.sum(grad_picked * picked, axis=1) * factor
    grad_powers = (
        jnp.einsum("re,ke->rk", grad_weighted, codes, preferred_element_type=jnp.float32)
        + grad_total[:, None]
    )
    grad_scores = grad_powers * powers
    grad_inner = (2.0 * BETA * grad_scores).astype(jnp.bfloat16)
    grad_rows = jnp.einsum("rk,ke->re", grad_inner, codes, preferred_element_type=jnp.float32)
    grad_codes = jnp.einsum(
        "rk,re->ke", powers.astype(jnp.bfloat16), grad_weighted, preferred_element_type=jnp.float32
    )
    grad_codes = grad_codes + jnp.einsum(
        "rk,re->ke", grad_inner, rows_low, preferred_element_type=jnp.float32
    )
    grad_codes = grad_codes - 2.0 * BETA * codes_wide * jnp.sum(grad_scores, axis=0)[:, None]
    counts = jnp.sum(powers * (weight * factor)[:, None], axis=0)
    return (grad_rows, grad_codes, counts)


def nesterov_step(master, moment, average, grad, rate):
    moment_new = MOMENTUM * moment + grad
    master_new = master - rate * (grad + MOMENTUM * moment_new)
    return (moment_new, master_new, AVERAGE_DECAY * average + (1.0 - AVERAGE_DECAY) * master_new)


def body(
    crops_in,
    crop_weight,
    cotangent,
    conv_copy,
    down_copy,
    proj_copy,
    norm_copy,
    codebook,
    conv_master,
    conv_moment,
    conv_average,
    down_master,
    down_moment,
    down_average,
    proj_master,
    proj_moment,
    proj_average,
    norm_master,
    norm_moment,
    norm_average,
    code_master,
    code_moment,
    code_average,
    repl_code,
    repl_src,
):
    dp_count = lax.axis_size("dp")
    code_count = lax.axis_size("code")
    local = lax.all_to_all(crops_in, "dp", split_axis=1, concat_axis=2, tiled=True)[0]
    crop_dev, pixels, channels = local.shape
    side = math.isqrt(pixels)
    half = side // 2
    positions = half * half
    width = proj_copy.shape[1]
    code_dev = codebook.shape[0]
    inputs = local.astype(jnp.float32)
    gains = norm_copy.astype(jnp.float32)
    out_first, normed_first, inverse_first = group_norm(inputs, gains[:, 0], gains[:, 1])
    act_first = jax.nn.silu(out_first).astype(jnp.bfloat16)
    conv_first = conv_forward(act_first, conv_copy[:, 0], side)
    out_second, normed_second, inverse_second = group_norm(conv_first, gains[:, 2], gains[:, 3])
    act_second = jax.nn.silu(out_second).astype(jnp.bfloat16)
    conv_second = conv_forward(act_second, conv_copy[:, 1], side)
    summed = (inputs + conv_second).astype(jnp.bfloat16)
    reduced = down_forward(summed, down_copy, side).astype(jnp.bfloat16)
    latent = jnp.einsum(
        "blc,ce->ble", reduced, proj_copy, preferred_element_type=jnp.float32
    ).astype(jnp.bfloat16)
    group_latent, group_weight, group_cot = (
        lax.all_gather(latent[None], "code", axis=0, tiled=True),
        lax.all_gather(crop_weight, "code", axis=0, tiled=True),
        lax.all_gather(cotangent, "code", axis=0, tiled=True),
    )
    rows_count = code_count * crop_dev * positions
    block = 512
    blocks = rows_count // block
    residual = group_latent.reshape(rows_count, width).astype(jnp.float32)
    token_weight = jnp.broadcast_to(
        group_weight.astype(jnp.float32)[:, :, None], (code_count, crop_dev, positions)
    ).reshape(rows_count)
    cot_rows = group_cot.reshape(rows_count, width).astype(jnp.float32)
    codes_wide = codebook.astype(jnp.float32)
    norms = jnp.sum(codes_wide * codes_wide, axis=1)

    def forward_block(piece):
        return soft_forward(piece, codebook, norms)

    quantized = jnp.zeros((rows_count, width), jnp.float32)
    levels = []
    kept = []
    for level in range(DEPTH):
        levels.append(residual)
        rows_low = residual.astype(jnp.bfloat16)
        peak_part, total_part, weighted_part = lax.map(
            forward_block, rows_low.reshape(blocks, block, width)
        )
        peak_part = peak_part.reshape(rows_count)
        total_part = total_part.reshape(rows_count)
        weighted_part = weighted_part.reshape(rows_count, width)
        peak_all, total_all, weighted_all = combined_all(
            (peak_part, total_part, weighted_part), "code", combine_soft
        )
        picked = weighted_all / total_all[:, None]
        kept.append((peak_part, jnp.exp(peak_part - peak_all), 1.0 / total_all, picked))
        residual = residual - picked
        quantized = quantized + picked
    set_index = lax.axis_index("code")
    own_start = set_index * crop_dev * positions
    quantized_own = lax.dynamic_slice_in_dim(quantized, own_start, crop_dev * positions, 0)

    def back_step(state, piece):
        grad_rows, grad_piece, count_piece = soft_backward(
            piece[0],
            piece[1],
            piece[2],
            piece[3],
            piece[4],
            piece[5],
            piece[6],
            codebook,
            codes_wide,
            norms,
        )
        return ((state[0] + grad_piece, state[1] + count_piece), grad_rows)

    carry = 2.0 * COMMIT * token_weight[:, None] * residual
    grad_codes = jnp.zeros((code_dev, width), jnp.float32)
    counts = jnp.zeros((code_dev,), jnp.float32)
    for level in reversed(range(DEPTH)):
        peak_part, scale_part, inverse_total, picked = kept[level]
        grad_picked = cot_rows - carry
        rows_low = levels[level].astype(jnp.bfloat16)
        pieces = (
            rows_low.reshape(blocks, block, width),
            peak_part.reshape(blocks, block),
            scale_part.reshape(blocks, block),
            inverse_total.reshape(blocks, block),
            grad_picked.reshape(blocks, block, width),
            picked.reshape(blocks, block, width),
            token_weight.reshape(blocks, block),
        )
        (grad_codes, counts), grad_rows = lax.scan(back_step, (grad_codes, counts), pieces)
        carry = carry + lax.psum(
            grad_rows.reshape(rows_count, width).astype(jnp.bfloat16), "code"
        ).astype(jnp.float32)
        if level > 0:
            carry = carry + 2.0 * COMMIT * token_weight[:, None] * levels[level]
    grad_latent = lax.dynamic_slice_in_dim(carry, own_start, crop_dev * positions, 0)
    grad_latent = grad_latent.reshape(crop_dev, positions, width).astype(jnp.bfloat16)
    grad_proj = jnp.einsum("blc,ble->ce", reduced, grad_latent, preferred_element_type=jnp.float32)
    grad_reduced = jnp.einsum(
        "ble,ce->blc", grad_latent, proj_copy, preferred_element_type=jnp.float32
    ).astype(jnp.bfloat16)
    grad_summed, grad_down = down_backward(summed, grad_reduced, down_copy, side)
    grad_act_second, conv_grad_second = conv_backward(
        act_second, grad_summed.astype(jnp.bfloat16), conv_copy[:, 1], side
    )
    grad_out_second = grad_act_second * silu_slope(out_second)
    grad_conv_first, gain_second, bias_second = group_back(
        grad_out_second, normed_second, inverse_second, gains[:, 2]
    )
    grad_act_first, conv_grad_first = conv_backward(
        act_first, grad_conv_first.astype(jnp.bfloat16), conv_copy[:, 0], side
    )
    grad_out_first = grad_act_first * silu_slope(out_first)
    grad_branch, gain_first, bias_first = group_back(
        grad_out_first, normed_first, inverse_first, gains[:, 0]
    )
    input_grad = grad_summed + grad_branch
    input_back = lax.all_to_all(
        input_grad[None].astype(jnp.bfloat16), "dp", split_axis=2, concat_axis=1, tiled=True
    ).astype(jnp.float32)
    conv_flat = jnp.stack([conv_grad_first, conv_grad_second], axis=1).reshape(
        channels, 18, channels
    )
    proj_flat = grad_proj.reshape(channels, 1, width)
    conv_part, down_part, proj_part = (
        lax.psum_scatter(
            conv_flat.astype(jnp.bfloat16), "dp", scatter_dimension=0, tiled=True
        ).astype(jnp.float32),
        lax.psum_scatter(
            grad_down.astype(jnp.bfloat16), "dp", scatter_dimension=0, tiled=True
        ).astype(jnp.float32),
        lax.psum_scatter(
            proj_flat.astype(jnp.bfloat16), "dp", scatter_dimension=0, tiled=True
        ).astype(jnp.float32),
    )
    conv_part, down_part, proj_part = (
        lax.psum_scatter(
            conv_part.astype(jnp.bfloat16), "code", scatter_dimension=2, tiled=True
        ).astype(jnp.float32),
        lax.psum_scatter(
            down_part.astype(jnp.bfloat16), "code", scatter_dimension=2, tiled=True
        ).astype(jnp.float32),
        lax.psum_scatter(
            proj_part.astype(jnp.bfloat16), "code", scatter_dimension=2, tiled=True
        ).astype(jnp.float32),
    )
    norm_grad = lax.psum(
        jnp.stack([gain_first, bias_first, gain_second, bias_second], axis=1), ("dp", "code")
    )
    crops_set = crop_dev * dp_count
    flat_src = repl_src.reshape(-1)
    set_id = flat_src // (crops_set * positions)
    crop_id = flat_src // positions % crops_set
    mine = crop_id // crop_dev == lax.axis_index("dp")
    row_id = (set_id * crop_dev + crop_id % crop_dev) * positions + flat_src % positions
    depth_id = jnp.repeat(jnp.arange(DEPTH, dtype=jnp.int32), repl_src.shape[1])
    level_stack = jnp.stack(levels)
    picked_rows = jnp.where(mine[:, None], level_stack[depth_id, row_id], 0.0)
    code_grad, source_rows = (
        lax.psum_scatter(
            grad_codes.astype(jnp.bfloat16), "dp", scatter_dimension=1, tiled=True
        ).astype(jnp.float32),
        lax.psum_scatter(
            picked_rows.astype(jnp.bfloat16), "dp", scatter_dimension=1, tiled=True
        ).astype(jnp.float32),
    )
    counts_all = lax.psum(counts, "dp")
    pixels_all = crop_dev * pixels * dp_count * code_count
    weight_rate = WEIGHT_RATE / math.sqrt(pixels_all)
    norm_rate = NORM_RATE / math.sqrt(pixels_all)
    codes_all = code_dev * code_count
    crops_all = crop_dev * dp_count * code_count
    code_rate = CODE_RATE / math.sqrt(
        DEPTH * crop_dev * positions * dp_count * code_count / codes_all
    )
    conv_out = nesterov_step(
        conv_master, conv_moment, conv_average, conv_part.reshape(conv_master.shape), weight_rate
    )
    down_out = nesterov_step(down_master, down_moment, down_average, down_part, weight_rate)
    proj_out = nesterov_step(
        proj_master, proj_moment, proj_average, proj_part.reshape(proj_master.shape), weight_rate
    )
    norm_out = nesterov_step(norm_master, norm_moment, norm_average, norm_grad, norm_rate)
    mean_count = DEPTH * positions * crops_all / codes_all
    share = mean_count / (mean_count + counts_all)
    code_load = counts_all / mean_count
    code_moment_new = MOMENTUM * code_moment + code_grad
    stepped = code_master - code_rate * (code_grad + MOMENTUM * code_moment_new)
    start = lax.axis_index("code") * code_dev
    select = (
        repl_code.reshape(-1)[:, None] - start == jnp.arange(code_dev, dtype=jnp.int32)[None, :]
    ).astype(jnp.float32)
    share_rows = jnp.dot(select, share, precision=HIGH)
    old_rows = jnp.dot(select, stepped, precision=HIGH)
    delta = share_rows[:, None] * (source_rows - old_rows)
    code_master_new = stepped + jnp.dot(select.T, delta, precision=HIGH)
    code_average_new = AVERAGE_DECAY * code_average + (1.0 - AVERAGE_DECAY) * code_master_new
    return (
        quantized_own.reshape(1, crop_dev, positions, width),
        input_back,
        conv_out[0],
        conv_out[1],
        conv_out[2],
        down_out[0],
        down_out[1],
        down_out[2],
        proj_out[0],
        proj_out[1],
        proj_out[2],
        norm_out[0],
        norm_out[1],
        norm_out[2],
        code_moment_new,
        code_master_new,
        code_average_new,
        code_load,
    )


def solution(mesh):
    in_specs = (
        P("code", None, "dp", None),
        P("code", "dp"),
        P("code", "dp", None, None),
        P(),
        P(),
        P(),
        P(),
        P("code", None),
        P("dp", None, None, "code"),
        P("dp", None, None, "code"),
        P("dp", None, None, "code"),
        P("dp", None, "code"),
        P("dp", None, "code"),
        P("dp", None, "code"),
        P("dp", "code"),
        P("dp", "code"),
        P("dp", "code"),
        P(),
        P(),
        P(),
        P("code", "dp"),
        P("code", "dp"),
        P("code", "dp"),
        P(),
        P(),
    )
    out_specs = (
        P("code", "dp", None, None),
        P("code", None, "dp", None),
        P("dp", None, None, "code"),
        P("dp", None, None, "code"),
        P("dp", None, None, "code"),
        P("dp", None, "code"),
        P("dp", None, "code"),
        P("dp", None, "code"),
        P("dp", "code"),
        P("dp", "code"),
        P("dp", "code"),
        P(),
        P(),
        P(),
        P("code", "dp"),
        P("code", "dp"),
        P("code", "dp"),
        P("code"),
    )
    return jax.shard_map(body, mesh=mesh, in_specs=in_specs, out_specs=out_specs, check_vma=False)
```

profile of v0, /device:TPU:0, one launch (start us, length us, event | category | flops | bytes accessed | tf_op | source)
XLA Modules:
  0.0 1055.5 jit_solution(6226880119043020393)
XLA Ops:
  7.2 7.4 all-to-all-start
  18.1 19.5 %fusion.241 = (bf16[512,1,9,512]{3,1,2,0:T(2,128)(2,1)S(1)}, bf16[512,1,9,512]{3,1,2,0:T(2,128)(2,1)}) fusion(bf16[512,2,9,512]{3,1,2,0:T(2,128)(2,1)} %param.36), kind=kLoop, calls=%fused_computation.551 | loop fusion | bytes 18874368 | tf_op jit(solution)/shard_map/slice | solution.py:234
  37.6 9.1 copy_bitcast_fusion
  78.0 8.2 slice.326
  86.2 8.2 slice.324
  94.4 8.2 slice.322
  102.7 6.2 slice.320
  149.5 12.3 %while.48 = (s32[]{:T(128)}, f32[512]{0:T(512)}, f32[512]{0:T(512)}, f32[512,256]{1,0:T(8,128)}, bf16[4,512]{1,0:T(4,128)(2,1)}, /*index=5*/bf16[4,512]{1,0:T(4,...) while((s32[]{:T(128)}, f32[512]{0:T(512)}, f32[512]{0:T(512)}, ...), condition=%wide.region_12.13_spmd, body=%wide.region_11.12_spmd.sunk | while | flops 528389 | bytes 1337487 | solution.py:33
  192.3 12.3 %while.49 = (s32[]{:T(128)}, f32[512]{0:T(512)}, f32[512]{0:T(512)}, f32[512,256]{1,0:T(8,128)}, bf16[4,512]{1,0:T(4,128)(2,1)}, /*index=5*/bf16[4,512]{1,0:T(4,...) while((s32[]{:T(128)}, f32[512]{0:T(512)}, f32[512]{0:T(512)}, ...), condition=%wide.region_16.17_spmd, body=%wide.region_15.16_spmd.sunk | while | flops 528389 | bytes 1337487 | solution.py:33
  234.6 12.3 %while.50 = (s32[]{:T(128)}, f32[512]{0:T(512)}, f32[512]{0:T(512)}, f32[512,256]{1,0:T(8,128)}, bf16[4,512]{1,0:T(4,128)(2,1)}, /*index=5*/bf16[4,512]{1,0:T(4,...) while((s32[]{:T(128)}, f32[512]{0:T(512)}, f32[512]{0:T(512)}, ...), condition=%wide.region_20.21_spmd, body=%wide.region_19.20_spmd.sunk | while | flops 528389 | bytes 1337487 | solution.py:33
  269.7 7.1 all_gather.71
  296.6 12.4 %while.51 = (s32[]{:T(128)}, f32[512]{0:T(512)}, f32[512]{0:T(512)}, f32[512,256]{1,0:T(8,128)}, bf16[4,512]{1,0:T(4,128)(2,1)}, /*index=5*/bf16[4,512]{1,0:T(4,...) while((s32[]{:T(128)}, f32[512]{0:T(512)}, f32[512]{0:T(512)}, ...), condition=%wide.region_24.25_spmd, body=%wide.region_23.24_spmd.sunk | while | flops 528389 | bytes 1337487 | solution.py:33
  314.1 6.2 fusion.245
  325.8 33.0 %all-reduce.9.cloned.1.call-done = bf16[512,256]{1,0:T(8,128)(2,1)} async-done(((bf16[512,256]{1,0:T(8,128)(2,1)}), bf16[512,256]{1,0:T(8,128)(2,1)}) %all-reduce.9.cloned.1.call-update) | async-done | bytes 262160 | tf_op jit(solution)/shard_map/psum | solution.py:317
  374.3 32.1 %all-reduce.11.cloned.1.call-done = bf16[512,256]{1,0:T(8,128)(2,1)} async-done(((bf16[512,256]{1,0:T(8,128)(2,1)}), bf16[512,256]{1,0:T(8,128)(2,1)}) %all-reduce.11.cloned.1.call-update) | async-done | bytes 262160 | tf_op jit(solution)/shard_map/psum | solution.py:317
  421.8 31.9 %all-reduce.13.cloned.1.call-done = bf16[512,256]{1,0:T(8,128)(2,1)} async-done(((bf16[512,256]{1,0:T(8,128)(2,1)}), bf16[512,256]{1,0:T(8,128)(2,1)}) %all-reduce.13.cloned.1.call-update) | async-done | bytes 262160 | tf_op jit(solution)/shard_map/psum | solution.py:317
  469.0 32.1 %all-reduce.15.cloned.1.call-done = bf16[512,256]{1,0:T(8,128)(2,1)} async-done(((bf16[512,256]{1,0:T(8,128)(2,1)}), bf16[512,256]{1,0:T(8,128)(2,1)}) %all-reduce.15.cloned.1.call-update) | async-done | bytes 262160 | tf_op jit(solution)/shard_map/psum | solution.py:317
  560.1 8.3 pad_maximum_fusion
  575.5 7.3 fusion.8
  582.8 8.1 fusion.26
  591.0 7.6 fusion.14
  603.2 7.7 fusion.13
  618.1 9.0 fusion.15
  631.5 15.0 %multiply_reduce_fusion.2 = (f32[4096]{0:T(1024)S(1)}, f32[4096]{0:T(1024)S(1)}, f32[4096]{0:T(1024)S(1)}, f32[4096]{0:T(1024)S(1)}) fusion(f32[512]{0:T(512)S(1)} %copy-done.99, f32[512]{0:T(512)S(1)} %copy-done.69, f32[4096]{0:T(1024)S(1)} %fusion.16, f32[512,4096]{1,0:T(8,128)} %copy-done.4, f32[512]{0:T(512)S(1)} %copy-done.100, f32[512]{0:T(512)S(1)} %copy-done.72, ...), kind=kLoop, calls=%fused_computation.32 | loop fusion | flops 50315264 | bytes 33652736 | tf_op jit(solution)/shard_map/while/body/eval_jaxpr/reduce_sum | solution.py:184
  646.5 38.8 %psum.47 = f32[4096]{0:T(1024)S(1)} all-reduce(f32[4096]{0:T(1024)S(1)} %add_add_fusion), channel_id=1, replica_groups=mesh['dp'=8,'code'=4] {'dp'}, use_global_device_ids=true, to_apply=%region_61.62 | all-reduce | flops 4096 | bytes 32768 | tf_op jit(solution)/shard_map/psum | solution.py:393
  719.2 44.4 %psum.46 = f32[512,4]{0,1:T(4,128)S(1)} all-reduce(f32[512,4]{0,1:T(4,128)S(1)} %pad_maximum_fusion.4), channel_id=1, replica_groups=mesh['dp'=8,'code'=4] {'dp','code'}, use_global_device_ids=true, to_apply=%region_51.52 | all-reduce | flops 2048 | bytes 16384 | tf_op jit(solution)/shard_map/psum | solution.py:373
  763.5 70.8 %reduce-scatter.15.cloned.1.call-done = bf16[64,18,512]{2,0,1:T(8,128)(2,1)} async-done(((bf16[512,18,512]{2,0,1:T(8,128)(2,1)}), bf16[64,18,512]{2,0,1:T(8,128)(2,1)}) %reduce-scatter.15.cloned.1.call-update) | async-done | bytes 1179664 | tf_op jit(solution)/shard_map/reduce_scatter | solution.py:352
  841.4 14.3 %reduce-scatter.29.cloned.1.call-done = bf16[64,64]{1,0:T(8,128)(2,1)} async-done(((bf16[256,64]{1,0:T(8,128)(2,1)}), bf16[64,64]{1,0:T(8,128)(2,1)}) %reduce-scatter.29.cloned.1.call-update) | async-done | bytes 8208
  859.8 67.6 %reduce-scatter.21.cloned.1.call-done = bf16[4096,32]{0,1:T(8,128)(2,1)} async-done(((bf16[4096,256]{0,1:T(8,128)(2,1)}), bf16[4096,32]{0,1:T(8,128)(2,1)}) %reduce-scatter.21.cloned.1.call-update) | async-done | bytes 262160 | tf_op jit(solution)/shard_map/reduce_scatter | solution.py:386
  928.6 62.8 %reduce-scatter.23.cloned.1.call-done = bf16[256,32]{0,1:T(8,128)(2,1)} async-done(((bf16[256,256]{0,1:T(8,128)(2,1)}), bf16[256,32]{0,1:T(8,128)(2,1)}) %reduce-scatter.23.cloned.1.call-update) | async-done | bytes 16400 | tf_op jit(solution)/shard_map/reduce_scatter | solution.py:389
  998.5 15.0 %reduce-scatter.27.cloned.1.call-done = bf16[128,256]{1,0:T(8,128)(2,1)} async-done(((bf16[512,256]{1,0:T(8,128)(2,1)}), bf16[128,256]{1,0:T(8,128)(2,1)}) %reduce-scatter.27.cloned.1.call-update) | async-done | bytes 65552
  1017.8 23.8 %reduce-scatter.25.cloned.1.call-done = bf16[128,1152]{1,0:T(8,128)(2,1)} async-done(((bf16[512,1152]{1,0:T(8,128)(2,1)}), bf16[128,1152]{1,0:T(8,128)(2,1)}) %reduce-scatter.25.cloned.1.call-update) | async-done | bytes 294928
  (593 shorter events, 429.7 us)
Async XLA Ops:
  7.2 107.9 %copy-start = (bf16[512,256]{1,0:T(8,128)(2,1)S(1)}, bf16[512,256]{1,0:T(8,128)(2,1)}, u32[]{:S(2)}) copy-start(bf16[512,256]{1,0:T(8,128)(2,1)} %param.38) | copy-start | bytes 786436
  7.2 44.2 %all-to-all-start = ((bf16[1,16,32,512]{3,2,0,1:T(8,128)(2,1)}), bf16[1,16,32,512]{3,2,0,1:T(8,128)(2,1)S(1)}, u32[]{:S(2)}, u32[]{:S(2)}) async-start(bf16[1,16,32,512]{3,2,0,1:T(8,128)(2,1)} %bitcast.792), calls=%async_computation | async-start | bytes 1048576 | tf_op jit(solution)/shard_map/all_to_all | solution.py:223
  14.6 133.1 %all-gather.27.cloned.1.call-start = ((), (), s32[]{:S(2)}) async-start(), calls=%async_computation.19 | async-start | bytes 1310720 | tf_op jit(solution)/shard_map/all_gather | solution.py:25
  129.4 61.1 %all-gather.29.cloned.1.call-start = ((), (), s32[]{:S(2)}) async-start(), calls=%async_computation.20 | async-start | bytes 1310720 | tf_op jit(solution)/shard_map/all_gather | solution.py:25
  172.1 60.7 %all-gather.31.cloned.1.call-start = ((), (), s32[]{:S(2)}) async-start(), calls=%async_computation.21 | async-start | bytes 1310720 | tf_op jit(solution)/shard_map/all_gather | solution.py:25
  214.8 80.0 %all-gather.33.cloned.1.call-start = ((), (), s32[]{:S(2)}) async-start(), calls=%async_computation.22 | async-start | bytes 1310720 | tf_op jit(solution)/shard_map/all_gather | solution.py:25
  257.2 101.6 %all-reduce.9.cloned.1.call-start = ((), (), s32[]{:S(2)}) async-start(), calls=%async_computation.10 | async-start | bytes 524288 | tf_op jit(solution)/shard_map/psum | solution.py:317
  325.7 80.6 %all-reduce.11.cloned.1.call-start = ((), (), s32[]{:S(2)}) async-start(), calls=%async_computation.11 | async-start | bytes 524288 | tf_op jit(solution)/shard_map/psum | solution.py:317
  374.2 79.5 %all-reduce.13.cloned.1.call-start = ((), (), s32[]{:S(2)}) async-start(), calls=%async_computation.12 | async-start | bytes 524288 | tf_op jit(solution)/shard_map/psum | solution.py:317
  421.6 79.5 %all-reduce.15.cloned.1.call-start = ((), (), s32[]{:S(2)}) async-start(), calls=%async_computation.13 | async-start | bytes 524288 | tf_op jit(solution)/shard_map/psum | solution.py:317
  468.9 147.4 %reduce-scatter.19.cloned.1.call-start = ((), (), s32[]{:S(2)}) async-start(), calls=%async_computation.16 | async-start | bytes 294912 | tf_op jit(solution)/shard_map/reduce_scatter | solution.py:358
  520.6 184.8 %reduce-scatter.17.cloned.1.call-start = ((), (), s32[]{:S(2)}) async-start(), calls=%async_computation.15 | async-start | bytes 2359296 | tf_op jit(solution)/shard_map/reduce_scatter | solution.py:355
  549.8 284.6 %reduce-scatter.15.cloned.1.call-start = ((), (), s32[]{:S(2)}) async-start(), calls=%async_computation.14 | async-start | bytes 10616832 | tf_op jit(solution)/shard_map/reduce_scatter | solution.py:352
  568.5 287.2 %reduce-scatter.29.cloned.1.call-start = ((), (), s32[]{:S(2)}) async-start(), calls=%async_computation.25 | async-start | bytes 81920
  618.0 309.4 %reduce-scatter.21.cloned.1.call-start = ((), (), s32[]{:S(2)}) async-start(), calls=%async_computation.17 | async-start | bytes 2359296 | tf_op jit(solution)/shard_map/reduce_scatter | solution.py:386
  627.1 364.3 %reduce-scatter.23.cloned.1.call-start = ((), (), s32[]{:S(2)}) async-start(), calls=%async_computation.18 | async-start | bytes 147456 | tf_op jit(solution)/shard_map/reduce_scatter | solution.py:389
  631.4 382.1 %reduce-scatter.27.cloned.1.call-start = ((), (), s32[]{:S(2)}) async-start(), calls=%async_computation.24 | async-start | bytes 327680
  707.8 133.0 %copy-start.103 = (f32[512,4]{0,1:T(4,128)S(1)}, f32[512,4]{0,1:T(4,128)}, u32[]{:S(2)}) copy-start(f32[512,4]{0,1:T(4,128)} %param.52) | copy-start | bytes 24580
  707.8 133.0 %copy-start.104 = (f32[512,4]{0,1:T(4,128)S(1)}, f32[512,4]{0,1:T(4,128)}, u32[]{:S(2)}) copy-start(f32[512,4]{0,1:T(4,128)} %param.50) | copy-start | bytes 24580
  707.8 133.0 %copy-start.105 = (f32[512,4]{0,1:T(4,128)S(1)}, f32[512,4]{0,1:T(4,128)}, u32[]{:S(2)}) copy-start(f32[512,4]{0,1:T(4,128)} %param.51) | copy-start | bytes 24580
  707.8 148.8 %copy-start.91 = (f32[64,64]{1,0:T(8,128)S(1)}, f32[64,64]{1,0:T(8,128)}, u32[]{:S(2)}) copy-start(f32[64,64]{1,0:T(8,128)} %param.49) | copy-start | bytes 49156
  707.8 148.8 %copy-start.92 = (f32[64,64]{1,0:T(8,128)S(1)}, f32[64,64]{1,0:T(8,128)}, u32[]{:S(2)}) copy-start(f32[64,64]{1,0:T(8,128)} %param.47) | copy-start | bytes 49156
  707.8 148.8 %copy-start.93 = (f32[64,64]{1,0:T(8,128)S(1)}, f32[64,64]{1,0:T(8,128)}, u32[]{:S(2)}) copy-start(f32[64,64]{1,0:T(8,128)} %param.48) | copy-start | bytes 49156
  711.1 146.1 %all-to-all-start.1 = ((bf16[1,2,256,512]{3,1,0,2:T(2,128)(2,1)}), bf16[1,2,256,512]{3,1,0,2:T(2,128)(2,1)}, u32[]{:S(2)}, u32[]{:S(2)}) async-start(bf16[1,2,256,512]{3,1,0,2:T(2,128)(2,1)} %copy.240), calls=%async_computation.1 | async-start | bytes 1048576 | tf_op jit(solution)/shard_map/all_to_all | solution.py:344
  715.3 326.4 %reduce-scatter.25.cloned.1.call-start = ((), (), s32[]{:S(2)}) async-start(), calls=%async_computation.23 | async-start | bytes 1474560
  719.1 272.3 %copy-start.108 = (s32[256]{0:T(256)S(1)}, s32[256]{0:T(256)}, u32[]{:S(2)}) copy-start(s32[256]{0:T(256)} %copy-done.107) | copy-start | bytes 3076
  838.1 176.5 %copy-start.60 = (f32[64,4,128]{2,1,0:T(4,128)S(1)}, f32[64,4,128]{2,1,0:T(4,128)}, u32[]{:S(2)}) copy-start(f32[64,4,128]{2,1,0:T(4,128)} %param.46) | copy-start | bytes 393220
  840.8 154.0 %copy-start.55 = (f32[4096,32]{0,1:T(8,128)S(1)}, f32[4096,32]{0,1:T(8,128)}, u32[]{:S(2)}) copy-start(f32[4096,32]{0,1:T(8,128)} %param.55) | copy-start | bytes 1572868
  840.8 202.8 %copy-start.49 = (f32[64,2,9,128]{3,1,2,0:T(2,128)S(1)}, f32[64,2,9,128]{3,1,2,0:T(2,128)}, u32[]{:S(2)}) copy-start(f32[64,2,9,128]{3,1,2,0:T(2,128)} %param.43) | copy-start | bytes 1769476
  840.8 202.8 %copy-start.50 = (f32[64,2,9,128]{3,1,2,0:T(2,128)S(1)}, f32[64,2,9,128]{3,1,2,0:T(2,128)}, u32[]{:S(2)}) copy-start(f32[64,2,9,128]{3,1,2,0:T(2,128)} %param.42) | copy-start | bytes 1769476
  927.4 121.4 %copy-start.1 = (bf16[512,256]{1,0:T(8,128)(2,1)S(1)}, bf16[512,256]{1,0:T(8,128)(2,1)}, u32[]{:S(2)}) copy-start(bf16[512,256]{1,0:T(8,128)(2,1)} %param.38) | copy-start | bytes 786436
  928.6 120.1 %copy-start.40 = (f32[4096,32]{0,1:T(8,128)}, f32[4096,32]{0,1:T(8,128)S(1)}, u32[]{:S(2)}) copy-start(f32[4096,32]{0,1:T(8,128)S(1)} %convert_add_fusion.3) | copy-start | bytes 1572868
  (108 other events, 977.8 us)
Sparse Core Ops, SparseCore 0:
  129.6 18.1 all-gather.26
  172.2 17.8 all-gather.28
  215.0 17.8 all-gather.30
  257.3 17.6 all-gather.32
  325.9 32.9 all-reduce.8
  374.3 31.9 all-reduce.10
  421.7 31.9 all-reduce.12
  469.0 31.9 all-reduce.14
  520.7 61.2 reduce-scatter.18
  585.5 67.0 reduce-scatter.16
  656.1 178.1 reduce-scatter.14
  837.2 18.4 reduce-scatter.28
  859.7 67.6 reduce-scatter.20
  931.5 59.8 reduce-scatter.22
  994.4 19.0 reduce-scatter.26
  1015.9 25.7 reduce-scatter.24
where the time goes:
time: 1070 us; the launch traced here: 1060 us
  waiting for transfers between devices  384 us (36%)
  matrix products  204 us (19%)
  other arithmetic  149 us (14%)
  local copies, waits for them, and re-layouts  146 us (14%)
  blocking collectives  144 us (13%)
  between operations  16.2 us (2%)
  starting transfers between devices  13 us (1%)
    psum x4, waiting for transfers between devices, body(): lax.psum(grad_rows.reshape(rows_count, width).astype(jnp.bfloat16), 'code')  129 us
    reduce_scatter x1, waiting for transfers between devices, body(): lax.psum_scatter(conv_flat.astype(jnp.bfloat16), 'dp', scatter_dimension=...  70.8 us
    reduce_scatter x1, waiting for transfers between devices, body(): lax.psum_scatter(grad_codes.astype(jnp.bfloat16), 'dp', scatter_dimension...  67.6 us
    unnamed x279, local copies, waits for them, and re-layouts  63.7 us
    reduce_scatter x1, waiting for transfers between devices, body(): lax.psum_scatter(picked_rows.astype(jnp.bfloat16), 'dp', scatter_dimensio...  62.8 us
    unnamed x19, waiting for transfers between devices  53.4 us
    psum x1, blocking collectives, body(): lax.psum(jnp.stack([gain_first, bias_first, gain_second, bias_second], ax...  44.4 us
    all_gather x8, blocking collectives, combined_all(): lax.all_gather(part.astype(kind), axis)  41.9 us
  transfers between devices with their start and end apart: 18, of which 11 were waited for; matrix products, arithmetic and copies ran while one was open for 23% of the time, Pallas kernels for 0%

commit v1 on v0

v1 whole, which is shorter than its diff:
```python
import functools
import math

import jax
import jax.numpy as jnp
from jax import lax
from jax.experimental import pallas as pl
from jax.experimental.pallas import tpu as pltpu
from jax.sharding import PartitionSpec as P

GROUPS = 32
DEPTH = 4
BETA = 0.0625
EPSILON = 1e-05
MOMENTUM = 0.5
AVERAGE_DECAY = 0.5
COMMIT = 0.25
WEIGHT_RATE = 0.05
NORM_RATE = 0.5
CODE_RATE = 0.5

BF = jnp.bfloat16
F32 = jnp.float32
NT = (((1,), (1,)), ((), ()))
NN = (((1,), (0,)), ((), ()))
TN = (((0,), (0,)), ((), ()))
MIB = 1 << 20


def mm(a, b, dims=NN):
    return lax.dot_general(a, b, dims, preferred_element_type=F32)


def vmem():
    return pl.BlockSpec(memory_space=pltpu.VMEM)


def smem():
    return pl.BlockSpec(memory_space=pltpu.SMEM)


def hbm():
    return pl.BlockSpec(memory_space=pl.ANY)


def group_sum(rows, per_group):
    lanes = rows.shape[1]
    at = lax.broadcasted_iota(jnp.int32, rows.shape, 1)
    step = 1
    while step < per_group:
        up = pltpu.roll(rows, step, 1)
        down = pltpu.roll(rows, lanes - step, 1)
        rows = rows + jnp.where((at & step) != 0, up, down)
        step *= 2
    return rows


def col_sum(values):
    rows, lanes = values.shape
    return jnp.sum(jnp.sum(values.reshape(rows // 8, 8, lanes), axis=0), axis=0, keepdims=True)


def put_shifted(pad_ref, crop, lanes, values, side):
    pixels = values.shape[0]
    col = lax.broadcasted_iota(jnp.int32, values.shape, 0) % side
    left = jnp.where(col == 0, 0.0, pltpu.roll(values, 1, 0))
    right = jnp.where(col == side - 1, 0.0, pltpu.roll(values, pixels - 1, 0))
    for shift, grid in enumerate((left, values, right)):
        pad_ref[crop, shift, side : side + pixels, lanes] = grid.astype(BF)


def zero_borders(pad_ref, side):
    rows = pad_ref.shape[2]
    edge = jnp.zeros((side, pad_ref.shape[3]), BF)
    for crop in range(pad_ref.shape[0]):
        for shift in range(3):
            pad_ref[crop, shift, 0:side, :] = edge
            pad_ref[crop, shift, rows - side : rows, :] = edge


def pixel_order(pixels, side):
    half = side // 2
    lat = half * half
    row = lax.broadcasted_iota(jnp.int32, (pixels, pixels), 0)
    col = lax.broadcasted_iota(jnp.int32, (pixels, pixels), 1)
    tap, pos = row // lat, row % lat
    at = (2 * (pos // half) + tap // 2) * side + 2 * (pos % half) + tap % 2
    return jnp.where(at == col, 1.0, 0.0).astype(BF)


def chunks(channels):
    return [slice(k, k + 128) for k in range(0, channels, 128)]


def norm_stats(read, crops, pixels, channels, per_group):
    count = float(pixels * per_group)
    result = []
    sums = [
        jnp.concatenate([col_sum(read(c, k)) for k in chunks(channels)], axis=1)
        for c in range(crops)
    ]
    means = [group_sum(s, per_group) * (1.0 / count) for s in sums]
    for c in range(crops):
        parts = []
        for k in chunks(channels):
            d = read(c, k) - means[c][:, k]
            parts.append(col_sum(d * d))
        spread = group_sum(jnp.concatenate(parts, axis=1), per_group) * (1.0 / count)
        result.append((means[c], lax.rsqrt(spread + EPSILON)))
    return result


def conv_apply(pad_ref, crop, w_ref, side, pixels):
    total = None
    for b in range(3):
        rows = jnp.concatenate(
            [pad_ref[crop, b, side * a : side * a + pixels, :] for a in range(3)], axis=1
        )
        part = None
        weight = jnp.concatenate([w_ref[3 * a + b] for a in range(3)], axis=0)
        part = mm(rows, weight)
        total = part if total is None else total + part
    return total


def forward_kernel(
    side,
    x_ref,
    norm_ref,
    w_hbm,
    dn_ref,
    pj_ref,
    conv_ref,
    stats_ref,
    sel_ref,
    red_ref,
    lat_ref,
    w_ref,
    pad_ref,
    sum_ref,
    sem,
):
    crops, pixels, channels = x_ref.shape
    per_group = channels // GROUPS
    copies = [pltpu.make_async_copy(w_hbm.at[k], w_ref.at[k], sem.at[k]) for k in range(2)]
    for copy in copies:
        copy.start()
    zero_borders(pad_ref, side)
    for stage in range(2):
        if stage == 0:

            def read(c, k):
                return x_ref[c, :, k].astype(F32)

        else:

            def read(c, k):
                return conv_ref[c, :, k]

        stats = norm_stats(read, crops, pixels, channels, per_group)
        for c in range(crops):
            mean, inverse = stats[c]
            stats_ref[c, 2 * stage : 2 * stage + 1, :] = mean
            stats_ref[c, 2 * stage + 1 : 2 * stage + 2, :] = inverse
            for k in chunks(channels):
                normed = (read(c, k) - mean[:, k]) * inverse[:, k]
                out = normed * norm_ref[2 * stage : 2 * stage + 1, k]
                out = out + norm_ref[2 * stage + 1 : 2 * stage + 2, k]
                put_shifted(pad_ref, c, k, out * jax.nn.sigmoid(out), side)
        copies[stage].wait()
        for c in range(crops):
            total = conv_apply(pad_ref, c, w_ref.at[stage], side, pixels)
            if stage == 0:
                conv_ref[c] = total
            else:
                sum_ref[c] = (x_ref[c].astype(F32) + total).astype(BF)
    order = pixel_order(pixels, side)
    lat = pixels // 4
    for c in range(crops):
        picked = mm(order, sum_ref[c]).astype(BF)
        for tap in range(4):
            sel_ref[tap, c * lat : (c + 1) * lat, :] = picked[tap * lat : (tap + 1) * lat]
    reduced = mm(sel_ref[0], dn_ref[0])
    for tap in range(1, 4):
        reduced = reduced + mm(sel_ref[tap], dn_ref[tap])
    reduced = reduced.astype(BF)
    red_ref[...] = reduced
    lat_ref[...] = mm(reduced, pj_ref[...]).astype(BF)


def forward_call(x, norm, w, dn, pj, side):
    crops, pixels, channels = x.shape
    tokens = crops * pixels // 4
    flops = 4 * crops * pixels * channels * channels * 9
    return pl.pallas_call(
        functools.partial(forward_kernel, side),
        out_shape=[
            jax.ShapeDtypeStruct((crops, pixels, channels), F32),
            jax.ShapeDtypeStruct((crops, 8, channels), F32),
            jax.ShapeDtypeStruct((4, tokens, channels), BF),
            jax.ShapeDtypeStruct((tokens, channels), BF),
            jax.ShapeDtypeStruct((tokens, pj.shape[1]), BF),
        ],
        in_specs=[vmem(), vmem(), hbm(), vmem(), vmem()],
        out_specs=[vmem()] * 5,
        scratch_shapes=[
            pltpu.VMEM(w.shape, BF),
            pltpu.VMEM((crops, 3, pixels + 2 * side, channels), BF),
            pltpu.VMEM((crops, pixels, channels), BF),
            pltpu.SemaphoreType.DMA((2,)),
        ],
        compiler_params=pltpu.CompilerParams(vmem_limit_bytes=44 * MIB),
        cost_estimate=pl.CostEstimate(
            flops=2 * flops, bytes_accessed=16 * MIB, transcendentals=crops * pixels * channels * 2
        ),
        name="residual_forward",
    )(x, norm, w, dn, pj)


TILE = 1024


def quant_kernel(
    n_shard,
    place_ref,
    lat_ref,
    norms_ref,
    weight_ref,
    cot_ref,
    *rest,
):
    shard_hbm = rest[:n_shard]
    q_ref, g_ref, rows_ref, extra_ref, grad_ref = rest[n_shard : n_shard + 5]
    code_ref, score_ref, stack_ref, res_ref, pick_ref, tot_ref, side_ref, acc_ref, count_ref, sem = (
        rest[n_shard + 5 :]
    )
    tokens, width = lat_ref.shape
    codes = code_ref.shape[0]
    shard = codes // n_shard
    copies = [
        pltpu.make_async_copy(
            shard_hbm[k], code_ref.at[pl.ds(k * shard, shard), :], sem.at[k]
        )
        for k in range(n_shard)
    ]
    for copy in copies:
        copy.start()

    def tiles(first, last, init, fn):
        def step(i, carry):
            return fn(pl.multiple_of(i * TILE, TILE), carry)

        return lax.fori_loop(first // TILE, last // TILE, step, init)

    def fold(values, combine):
        out = values[:, :128]
        for k in range(128, values.shape[1], 128):
            out = combine(out, values[:, k : k + 128])
        return out

    residual = lat_ref[...].astype(F32)
    quantized = jnp.zeros((tokens, width), F32)
    for level in range(DEPTH):
        res_ref[level] = residual
        low = residual.astype(BF)
        rows_ref[level] = low
        scaled = low * jnp.asarray(2.0 * BETA, BF)

        def score(at, best):
            s = mm(scaled, code_ref[pl.ds(at, TILE), :], NT) - norms_ref[:, pl.ds(at, TILE)]
            score_ref[:, pl.ds(at, TILE)] = s
            return jnp.maximum(best, fold(s, jnp.maximum))

        best = jnp.full((tokens, 128), -jnp.inf, F32)
        if level == 0:
            for k in range(n_shard):
                copies[k].wait()
                best = tiles(k * shard, (k + 1) * shard, best, score)
        else:
            best = tiles(0, codes, best, score)
        peak = jnp.max(best, axis=1, keepdims=True)
        acc_ref[...] = jnp.zeros((tokens, width), F32)

        def power(at, total):
            p = jnp.exp(score_ref[:, pl.ds(at, TILE)] - peak)
            low_p = p.astype(BF)
            stack_ref[level * tokens : (level + 1) * tokens, pl.ds(at, TILE)] = low_p
            acc_ref[...] += mm(low_p, code_ref[pl.ds(at, TILE), :])
            return total + fold(p, jnp.add)

        total = tiles(0, codes, jnp.zeros((tokens, 128), F32), power)
        inverse = 1.0 / jnp.sum(total, axis=1, keepdims=True)
        picked = acc_ref[...] * inverse
        pick_ref[level] = picked
        tot_ref[level] = jnp.broadcast_to(inverse, (tokens, 128))
        residual = residual - picked
        quantized = quantized + picked
    q_ref[...] = quantized

    weight = weight_ref[...]
    cot = cot_ref[...].astype(F32)
    count_ref[...] = jnp.zeros(count_ref.shape, F32)
    carry = 2.0 * COMMIT * weight * residual
    for level in reversed(range(DEPTH)):
        inverse = tot_ref[level][:, 0:1]
        grad = cot - carry
        down = (grad * inverse).astype(BF)
        total_grad = -jnp.sum(grad * pick_ref[level], axis=1, keepdims=True) * inverse
        share = weight * inverse
        side_ref[:, level * tokens : (level + 1) * tokens] = grad_t(down)
        side_ref[:, (DEPTH + level) * tokens : (DEPTH + level + 1) * tokens] = grad_t(
            rows_ref[level]
        )
        acc_ref[...] = jnp.zeros((tokens, width), F32)

        def back(at, nothing):
            codes_tile = code_ref[pl.ds(at, TILE), :]
            p = stack_ref[level * tokens : (level + 1) * tokens, pl.ds(at, TILE)].astype(F32)
            ds = (mm(down, codes_tile, NT) + total_grad) * p * (2.0 * BETA)
            inner = ds.astype(BF)
            stack_ref[
                (DEPTH + level) * tokens : (DEPTH + level + 1) * tokens, pl.ds(at, TILE)
            ] = inner
            acc_ref[...] += mm(inner, codes_tile)
            weighted = (p * share).reshape(tokens // 8, 8, TILE)
            count_ref[0, :, pl.ds(at, TILE)] += jnp.sum(weighted, axis=0)
            count_ref[1, :, pl.ds(at, TILE)] += jnp.sum(ds.reshape(tokens // 8, 8, TILE), axis=0)
            return nothing

        tiles(0, codes, 0, back)
        carry = carry + acc_ref[...]
        if level > 0:
            carry = carry + 2.0 * COMMIT * weight * res_ref[level]
    g_ref[...] = carry.astype(BF)
    extra_ref[0:1, :] = jnp.sum(count_ref[0], axis=0, keepdims=True)
    extra_ref[1:2, :] = jnp.sum(count_ref[1], axis=0, keepdims=True)

    n_row = grad_ref.shape[1]
    block = grad_ref.shape[2]
    place = place_ref[0]
    sub = 512
    for k in range(n_shard):

        def out(i, nothing):
            at = pl.multiple_of(i * sub, sub)
            part = mm(side_ref[...], stack_ref[:, pl.ds(k * shard + at, sub)]).astype(BF)
            for r in range(n_row):
                grad_ref[k, r ^ place, :, pl.ds(at, sub)] = part[r * block : (r + 1) * block]
            return nothing

        lax.fori_loop(0, shard // sub, out, 0)


def grad_t(values):
    return values.astype(F32).T.astype(BF)


def quant_call(place, latent, norms, weight, cot, shards, n_row):
    tokens, width = latent.shape
    n_shard = len(shards)
    shard = shards[0].shape[0]
    codes = n_shard * shard
    return pl.pallas_call(
        functools.partial(quant_kernel, n_shard),
        out_shape=[
            jax.ShapeDtypeStruct((tokens, width), F32),
            jax.ShapeDtypeStruct((tokens, width), BF),
            jax.ShapeDtypeStruct((DEPTH, tokens, width), BF),
            jax.ShapeDtypeStruct((2, codes), F32),
            jax.ShapeDtypeStruct((n_shard, n_row, width // n_row, shard), BF),
        ],
        in_specs=[smem(), vmem(), vmem(), vmem(), vmem()] + [hbm()] * n_shard,
        out_specs=[vmem()] * 5,
        scratch_shapes=[
            pltpu.VMEM((codes, width), BF),
            pltpu.VMEM((tokens, codes), F32),
            pltpu.VMEM((2 * DEPTH * tokens, codes), BF),
            pltpu.VMEM((DEPTH, tokens, width), F32),
            pltpu.VMEM((DEPTH, tokens, width), F32),
            pltpu.VMEM((DEPTH, tokens, 128), F32),
            pltpu.VMEM((width, 2 * DEPTH * tokens), BF),
            pltpu.VMEM((tokens, width), F32),
            pltpu.VMEM((2, 8, codes), F32),
            pltpu.SemaphoreType.DMA((n_shard,)),
        ],
        compiler_params=pltpu.CompilerParams(vmem_limit_bytes=63 * MIB),
        cost_estimate=pl.CostEstimate(
            flops=48 * tokens * width * codes,
            bytes_accessed=18 * MIB,
            transcendentals=DEPTH * tokens * codes,
        ),
        name="soft_quantize",
    )(place, latent, norms, weight, cot, *shards)


def slope(values):
    sigma = jax.nn.sigmoid(values)
    return sigma * (1.0 + values * (1.0 - sigma))


def put_blocks(place_ref, outs, n_in, n_out, row, value):
    if len(outs) == 1:
        outs[0][row : row + value.shape[0], :] = value.astype(BF)
        return
    rows = value.shape[0] // n_in
    odd = place_ref[1] % 2 == 1
    line = place_ref[1] // 2
    low = value.astype(BF)
    for pair in range(n_out // 2):
        even = low[:, 256 * pair : 256 * pair + 128]
        other = low[:, 256 * pair + 128 : 256 * pair + 256]
        keep = jnp.where(odd, other, even)
        send = jnp.where(odd, even, other)
        for i in range(n_in):
            at = slice(i * rows, (i + 1) * rows)
            outs[0][pair ^ line, i ^ place_ref[0], row : row + rows, :] = keep[at]
            outs[1][pair ^ line, i ^ place_ref[0], row : row + rows, :] = send[at]


def put_proj(place_ref, outs, n_in, n_out, row, value):
    if len(outs) == 1:
        outs[0][row : row + value.shape[0], 0 : value.shape[1]] = value.astype(BF)
        outs[0][row : row + value.shape[0], value.shape[1] :] = jnp.zeros(value.shape, BF)
        return
    channels, width = value.shape
    rows = channels // n_in
    cols = width // n_out
    folded = []
    for i in range(n_in):
        top = value[i * rows : i * rows + rows // 2]
        low = value[i * rows + rows // 2 : (i + 1) * rows]
        folded.append(
            jnp.concatenate(
                [
                    part[:, c * cols : (c + 1) * cols]
                    for c in range(n_out)
                    for part in (top, low)
                ],
                axis=1,
            )
        )
    put_blocks(place_ref, outs, n_in, n_out, row, jnp.concatenate(folded, axis=0))


def norm_back(grad, normed, inverse, gain, per_group, count):
    dn = grad * gain
    first = group_sum(col_sum(dn), per_group) * (1.0 / count)
    second = group_sum(col_sum(dn * normed), per_group) * (1.0 / count)
    return inverse * (dn - first - normed * second)


def conv_back_image(pad_ref, crop, w_ref, side, pixels):
    total = None
    for tap in range(9):
        a, b = tap // 3, tap % 3
        rows = pad_ref[crop, 2 - b, side * (2 - a) : side * (2 - a) + pixels, :]
        part = mm(rows, w_ref[tap], NT)
        total = part if total is None else total + part
    return total


def conv_back_weight(pad_ref, crops, grad, side, pixels, store):
    for tap in range(9):
        a, b = tap // 3, tap % 3
        rows = jnp.concatenate(
            [pad_ref[c, b, side * a : side * a + pixels, :] for c in range(crops)], axis=0
        )
        store(tap, mm(rows, grad, TN))


def act_shifted(pad_ref, read, stats_ref, norm_ref, stage, crops, channels, side):
    for c in range(crops):
        for k in chunks(channels):
            normed = (read(c, k) - stats_ref[c, 2 * stage : 2 * stage + 1, k]) * stats_ref[
                c, 2 * stage + 1 : 2 * stage + 2, k
            ]
            out = normed * norm_ref[2 * stage : 2 * stage + 1, k]
            out = out + norm_ref[2 * stage + 1 : 2 * stage + 2, k]
            put_shifted(pad_ref, c, k, out * jax.nn.sigmoid(out), side)


def act_back(read, dact_ref, stats_ref, norm_ref, stage, crops, pixels, channels, grads_ref, store):
    per_group = channels // GROUPS
    count = float(pixels * per_group)
    for k in chunks(channels):
        gain_row = norm_ref[2 * stage : 2 * stage + 1, k]
        bias_row = norm_ref[2 * stage + 1 : 2 * stage + 2, k]
        grad_gain = jnp.zeros((1, 128), F32)
        grad_bias = jnp.zeros((1, 128), F32)
        for c in range(crops):
            inverse = stats_ref[c, 2 * stage + 1 : 2 * stage + 2, k]
            normed = (read(c, k) - stats_ref[c, 2 * stage : 2 * stage + 1, k]) * inverse
            dout = dact_ref[c, :, k] * slope(normed * gain_row + bias_row)
            grad_gain = grad_gain + col_sum(dout * normed)
            grad_bias = grad_bias + col_sum(dout)
            store(c, k, norm_back(dout, normed, inverse, gain_row, per_group, count))
        grads_ref[0:1, k] = grad_gain
        grads_ref[1:2, k] = grad_bias


def second_kernel(
    side,
    n_out_refs,
    n_in,
    n_out,
    place_ref,
    dlat_ref,
    red_ref,
    sel_ref,
    dn_ref,
    pj_ref,
    conv_ref,
    stats_ref,
    norm_ref,
    w_hbm,
    *rest,
):
    outs = rest[:n_out_refs]
    dsum_ref, dconv_ref, ngrad_ref, w_ref, apad_ref, dpad_ref, dact_ref, sem = rest[n_out_refs:]
    crops, pixels, channels = conv_ref.shape
    copy = pltpu.make_async_copy(w_hbm.at[1], w_ref, sem.at[0])
    copy.start()
    zero_borders(apad_ref, side)
    zero_borders(dpad_ref, side)
    rows = channels // n_in if n_out_refs == 2 else channels
    lat = pixels // 4

    def read(c, k):
        return conv_ref[c, :, k]

    dlat = dlat_ref[...]
    dred = mm(dlat, pj_ref[...], NT).astype(BF)
    order = pixel_order(pixels, side)
    pieces = [mm(dred, dn_ref[tap], NT).astype(BF) for tap in range(4)]
    for c in range(crops):
        mixed = jnp.concatenate([p[c * lat : (c + 1) * lat] for p in pieces], axis=0)
        dsum_ref[c] = mm(order, mixed, TN).astype(BF)
        for k in chunks(channels):
            put_shifted(dpad_ref, c, k, dsum_ref[c, :, k].astype(F32), side)
    copy.wait()
    for c in range(crops):
        dact_ref[c] = conv_back_image(dpad_ref, c, w_ref, side, pixels)

    def store(c, k, value):
        dconv_ref[c, :, k] = value.astype(BF)

    ngrad_ref[...] = jnp.zeros(ngrad_ref.shape, F32)
    act_back(read, dact_ref, stats_ref, norm_ref, 1, crops, pixels, channels, ngrad_ref, store)
    act_shifted(apad_ref, read, stats_ref, norm_ref, 1, crops, channels, side)
    grad = jnp.concatenate([dsum_ref[c] for c in range(crops)], axis=0)
    conv_back_weight(
        apad_ref,
        crops,
        grad,
        side,
        pixels,
        lambda tap, v: put_blocks(place_ref, outs, n_in, n_out, tap * rows, v),
    )
    for tap in range(4):
        put_blocks(place_ref, outs, n_in, n_out, (9 + tap) * rows, mm(sel_ref[tap], dred, TN))
    put_proj(place_ref, outs, n_in, n_out, 13 * rows, mm(red_ref[...], dlat, TN))


def first_weight_kernel(
    side, n_out_refs, n_in, n_out, place_ref, x_ref, stats_ref, norm_ref, dconv_ref, *rest
):
    outs = rest[:n_out_refs]
    (apad_ref,) = rest[n_out_refs:]
    crops, pixels, channels = x_ref.shape
    rows = channels // n_in if n_out_refs == 2 else channels
    zero_borders(apad_ref, side)

    def read(c, k):
        return x_ref[c, :, k].astype(F32)

    act_shifted(apad_ref, read, stats_ref, norm_ref, 0, crops, channels, side)
    grad = jnp.concatenate([dconv_ref[c] for c in range(crops)], axis=0)
    conv_back_weight(
        apad_ref,
        crops,
        grad,
        side,
        pixels,
        lambda tap, v: put_blocks(place_ref, outs, n_in, n_out, tap * rows, v),
    )


def first_image_kernel(
    side,
    n_part,
    place_ref,
    x_ref,
    stats_ref,
    norm_ref,
    dconv_ref,
    dsum_ref,
    w_hbm,
    *rest,
):
    part_refs = rest[:n_part]
    ngrad_ref, w_ref, dpad_ref, dact_ref, image_ref, sem = rest[n_part:]
    crops, pixels, channels = x_ref.shape
    copy = pltpu.make_async_copy(w_hbm.at[0], w_ref, sem.at[0])
    copy.start()
    zero_borders(dpad_ref, side)
    for c in range(crops):
        for k in chunks(channels):
            put_shifted(dpad_ref, c, k, dconv_ref[c, :, k].astype(F32), side)
    copy.wait()
    for c in range(crops):
        dact_ref[c] = conv_back_image(dpad_ref, c, w_ref, side, pixels)

    def read(c, k):
        return x_ref[c, :, k].astype(F32)

    def store(c, k, value):
        image_ref[c, :, k] = (value + dsum_ref[c, :, k].astype(F32)).astype(BF)

    ngrad_ref[...] = jnp.zeros(ngrad_ref.shape, F32)
    act_back(read, dact_ref, stats_ref, norm_ref, 0, crops, pixels, channels, ngrad_ref, store)
    span = pixels // n_part
    for k in range(n_part):
        if n_part == 1:
            part_refs[k][...] = image_ref[...]
        else:
            at = pl.multiple_of((place_ref[0] ^ k) * span, span)
            for c in range(crops):
                part_refs[k][c] = image_ref[c, pl.ds(at, span), :]


def conv_cost(crops, pixels, channels, convs):
    return pl.CostEstimate(
        flops=convs * 18 * crops * pixels * channels * channels,
        bytes_accessed=12 * MIB,
        transcendentals=crops * pixels * channels,
    )


def grad_shapes(halves, n_in, n_out, channels, units):
    if not halves:
        return [jax.ShapeDtypeStruct((units[0] * channels, channels), BF)]
    rows = channels // n_in
    shape = (n_out // 2, n_in, units[0] * rows + units[1], channels // n_out)
    return [jax.ShapeDtypeStruct(shape, BF)] * 2


def second_call(place, dlat, red, sel, dn, pj, conv, stats, norm, w, side, halves, n_in, n_out):
    crops, pixels, channels = conv.shape
    if halves:
        fold = channels // n_in * pj.shape[1] // channels
        grads = grad_shapes(True, n_in, n_out, channels, (13, fold))
    else:
        grads = grad_shapes(False, n_in, n_out, channels, (14, 0))
    pad = (crops, 3, pixels + 2 * side, channels)
    return pl.pallas_call(
        functools.partial(second_kernel, side, len(grads), n_in, n_out),
        out_shape=grads
        + [
            jax.ShapeDtypeStruct(conv.shape, BF),
            jax.ShapeDtypeStruct(conv.shape, BF),
            jax.ShapeDtypeStruct((8, channels), F32),
        ],
        in_specs=[smem()] + [vmem()] * 8 + [hbm()],
        out_specs=[vmem()] * (len(grads) + 3),
        scratch_shapes=[
            pltpu.VMEM(w.shape[1:], BF),
            pltpu.VMEM(pad, BF),
            pltpu.VMEM(pad, BF),
            pltpu.VMEM(conv.shape, F32),
            pltpu.SemaphoreType.DMA((1,)),
        ],
        compiler_params=pltpu.CompilerParams(vmem_limit_bytes=44 * MIB),
        cost_estimate=conv_cost(crops, pixels, channels, 2),
        name="second_backward",
    )(place, dlat, red, sel, dn, pj, conv, stats, norm, w)


def first_weight_call(place, x, stats, norm, dconv, side, halves, n_in, n_out):
    crops, pixels, channels = x.shape
    grads = grad_shapes(halves, n_in, n_out, channels, (9, 0))
    return pl.pallas_call(
        functools.partial(first_weight_kernel, side, len(grads), n_in, n_out),
        out_shape=grads,
        in_specs=[smem()] + [vmem()] * 4,
        out_specs=[vmem()] * len(grads),
        scratch_shapes=[pltpu.VMEM((crops, 3, pixels + 2 * side, channels), BF)],
        compiler_params=pltpu.CompilerParams(vmem_limit_bytes=44 * MIB),
        cost_estimate=conv_cost(crops, pixels, channels, 1),
        name="first_weight_backward",
    )(place, x, stats, norm, dconv)


def first_image_call(place, x, stats, norm, dconv, dsum, w, side, n_part):
    crops, pixels, channels = x.shape
    return pl.pallas_call(
        functools.partial(first_image_kernel, side, n_part),
        out_shape=[jax.ShapeDtypeStruct((crops, pixels // n_part, channels), BF)] * n_part
        + [jax.ShapeDtypeStruct((8, channels), F32)],
        in_specs=[smem()] + [vmem()] * 5 + [hbm()],
        out_specs=[vmem()] * (n_part + 1),
        scratch_shapes=[
            pltpu.VMEM(w.shape[1:], BF),
            pltpu.VMEM((crops, 3, pixels + 2 * side, channels), BF),
            pltpu.VMEM(x.shape, F32),
            pltpu.VMEM(x.shape, BF),
            pltpu.SemaphoreType.DMA((1,)),
        ],
        compiler_params=pltpu.CompilerParams(vmem_limit_bytes=44 * MIB),
        cost_estimate=conv_cost(crops, pixels, channels, 1),
        name="first_image_backward",
    )(place, x, stats, norm, dconv, dsum, w)


def swap(array, axis, bit):
    count = lax.axis_size(axis)
    return lax.ppermute(array, axis, [(i, i ^ bit) for i in range(count)])


def add_low(first, second):
    return (first.astype(F32) + second.astype(F32)).astype(BF)


ORDERS = (("x", "y", "z1", "z2"), ("y", "z1", "x", "z2"), ("z1", "x", "y", "z2"))
LINKS = {"x": ("code", 2), "y": ("dp", 1), "z1": ("dp", 2), "z2": ("dp", 4)}


def halve_all(part, order, dims):
    dims = list(dims)
    for name in order:
        if name not in dims:
            continue
        at = dims.index(name)
        axis, bit = LINKS[name]
        mine = lax.index_in_dim(part, 0, at, keepdims=False)
        theirs = lax.index_in_dim(part, 1, at, keepdims=False)
        part = add_low(mine, swap(theirs, axis, bit))
        dims.pop(at)
    return part


def thirds(total, unit):
    units = total // unit
    cuts = [0, (units + 2) // 3 * unit, (units + 2) // 3 * unit + (units + 1) // 3 * unit, total]
    return [(cuts[k], cuts[k + 1]) for k in range(3)]


def nesterov_step(master, moment, average, grad, rate):
    moment_new = MOMENTUM * moment + grad
    master_new = master - rate * (grad + MOMENTUM * moment_new)
    return (moment_new, master_new, AVERAGE_DECAY * average + (1.0 - AVERAGE_DECAY) * master_new)


def body(
    crops_in,
    crop_weight,
    cotangent,
    conv_copy,
    down_copy,
    proj_copy,
    norm_copy,
    codebook,
    conv_master,
    conv_moment,
    conv_average,
    down_master,
    down_moment,
    down_average,
    proj_master,
    proj_moment,
    proj_average,
    norm_master,
    norm_moment,
    norm_average,
    code_master,
    code_moment,
    code_average,
    repl_code,
    repl_src,
):
    dp_count = lax.axis_size("dp")
    code_count = lax.axis_size("code")
    dp_at = lax.axis_index("dp")
    code_at = lax.axis_index("code")
    halves = dp_count == 8 and code_count == 4
    place = jnp.stack([dp_at, code_at]).astype(jnp.int32)

    local = lax.all_to_all(crops_in, "dp", split_axis=1, concat_axis=2, tiled=True)[0]
    crop_dev, pixels, channels = local.shape
    side = math.isqrt(pixels)
    lat = pixels // 4
    tokens = crop_dev * lat
    width = proj_copy.shape[1]
    code_dev = codebook.shape[0]
    codes_all = code_dev * code_count

    codes_wide = codebook.astype(F32)
    norms = BETA * jnp.sum(codes_wide * codes_wide, axis=1)
    if halves:
        shards, norm_rows = [codebook], [norms]
        for bit in (1, 2, 3):
            shards.append(swap(codebook, "code", bit))
            norm_rows.append(swap(norms, "code", bit))
        norms_all = jnp.concatenate(norm_rows)
    else:
        every = lax.all_gather(codebook, "code", axis=0)
        shards = [every[k] for k in range(code_count)]
        norms_all = lax.all_gather(norms, "code", axis=0, tiled=True)

    w = conv_copy.transpose(1, 2, 0, 3)
    dn = down_copy.transpose(1, 0, 2)
    gains = norm_copy.T.astype(F32)
    conv1, stats, sel, reduced, latent = forward_call(local, gains, w, dn, proj_copy, side)

    weight_col = jnp.broadcast_to(
        crop_weight.astype(F32).reshape(crop_dev, 1), (crop_dev, lat)
    ).reshape(tokens, 1)
    n_row = dp_count if halves else 1
    place_q = place if halves else jnp.zeros_like(place)
    quantized, dlat, rows, extra, code_grads = quant_call(
        place_q,
        latent,
        norms_all.reshape(1, codes_all),
        weight_col,
        cotangent.reshape(tokens, width),
        shards,
        n_row,
    )

    second = second_call(
        place, dlat, reduced, sel, dn, proj_copy, conv1, stats, gains, w, side, halves, dp_count,
        code_count,
    )
    grads_second, (dsum, dconv, ngrad_second) = second[:-3], second[-3:]
    grads_first = first_weight_call(
        place, local, stats, gains, dconv, side, halves, dp_count, code_count
    )
    image = first_image_call(
        place, local, stats, gains, dconv, dsum, w, side, dp_count if halves else 1
    )
    image_parts, ngrad_first = image[:-1], image[-1]

    crops_set = crop_dev * dp_count
    flat_src = repl_src.reshape(-1)
    crop_id = flat_src // lat % crops_set
    owner = (crop_id // crop_dev == dp_at) & (flat_src // (crops_set * lat) == code_at)
    row_id = crop_id % crop_dev * lat + flat_src % lat
    depth_id = jnp.repeat(jnp.arange(DEPTH, dtype=jnp.int32), repl_src.shape[1])
    flat_rows = rows.reshape(DEPTH * tokens, width)
    pick = (
        jnp.where(owner, depth_id * tokens + row_id, -1)[:, None]
        == jnp.arange(DEPTH * tokens, dtype=jnp.int32)[None, :]
    ).astype(BF)
    source = mm(flat_rows, pick, (((0,), (1,)), ((), ()))).astype(BF)

    norm_grad = jnp.concatenate([ngrad_first[0:2], ngrad_second[0:2]], axis=0)

    if halves:
        def by_bits(array, lead):
            return array.reshape(array.shape[:lead] + (2, 2, 2) + array.shape[lead + 1 :])

        keep_own = add_low(code_grads[0], swap(code_grads[1], "code", 1))
        keep_far = add_low(code_grads[2], swap(code_grads[3], "code", 1))
        pieces = []
        for k, (low, high) in enumerate(thirds(code_dev, 128)):
            part = jnp.stack([keep_own[:, :, low:high], keep_far[:, :, low:high]])
            part = part.reshape((2, 2, 2, 2) + part.shape[2:])
            pieces.append(halve_all(part, ORDERS[k], ("x", "z2", "z1", "y")))
        code_grad = jnp.concatenate(pieces, axis=1).astype(F32)

        rows_x = extra.reshape(2, code_count, code_dev)
        near = rows_x[:, 0] + swap(rows_x[:, 1], "code", 1)
        far = rows_x[:, 2] + swap(rows_x[:, 3], "code", 1)
        sums = near + swap(far, "code", 2)
        for bit in (1, 2, 4):
            sums = sums + swap(sums, "dp", bit)

        start = dp_at * (width // dp_count)
        block = source.reshape(2, 2, 2, width // dp_count, source.shape[1])
        bits = [(dp_at >> 2) & 1, (dp_at >> 1) & 1, dp_at & 1]
        for bit, at in zip((4, 2, 1), bits):
            mine = lax.dynamic_index_in_dim(block, at, 0, keepdims=False)
            theirs = lax.dynamic_index_in_dim(block, 1 - at, 0, keepdims=False)
            block = add_low(mine, swap(theirs, "dp", bit))
        for bit in (1, 2):
            block = add_low(block, swap(block, "code", bit))
        source_rows = block

        def matrix(keep, send):
            total = add_low(keep, swap(send, "code", 1))
            total = total.reshape((2, 2, 2, 2) + total.shape[2:])
            pieces = []
            for k, (low, high) in enumerate(thirds(total.shape[4], 16)):
                pieces.append(
                    halve_all(total[:, :, :, :, low:high], ORDERS[k], ("x", "z2", "z1", "y"))
                )
            return jnp.concatenate(pieces, axis=0).astype(F32)

        rows_in = channels // dp_count
        out_dev = channels // code_count
        mat_second = matrix(*grads_second)
        mat_first = matrix(*grads_first)
        conv_part = jnp.stack(
            [
                mat_first.reshape(9, rows_in, out_dev),
                mat_second[: 9 * rows_in].reshape(9, rows_in, out_dev),
            ]
        ).transpose(2, 0, 1, 3)
        down_part = (
            mat_second[9 * rows_in : 13 * rows_in].reshape(4, rows_in, out_dev).transpose(1, 0, 2)
        )
        fold = mat_second[13 * rows_in :]
        proj_part = jnp.concatenate([fold[:, : out_dev // 2], fold[:, out_dev // 2 :]], axis=0)

        total = norm_grad
        for axis, bit in (("code", 1), ("code", 2), ("dp", 1), ("dp", 2), ("dp", 4)):
            total = total + swap(total, axis, bit)
        norm_grad = total

        parts = [image_parts[0]] + [swap(image_parts[k], "dp", k) for k in range(1, dp_count)]
        input_back = jnp.zeros((crop_dev * dp_count, pixels // dp_count, channels), F32)
        for k, part in enumerate(parts):
            input_back = lax.dynamic_update_slice(
                input_back, part.astype(F32), ((dp_at ^ k) * crop_dev, 0, 0)
            )
        input_back = input_back[None]
    else:
        flat = code_grads.reshape(code_count, width, code_dev)
        flat = lax.psum_scatter(flat, "code", scatter_dimension=0, tiled=True)[0]
        code_grad = lax.psum_scatter(flat, "dp", scatter_dimension=0, tiled=True).astype(F32)
        sums = lax.psum_scatter(extra, "code", scatter_dimension=1, tiled=True)
        sums = lax.psum(sums, "dp")
        source_rows = lax.psum_scatter(source, "dp", scatter_dimension=0, tiled=True)
        source_rows = lax.psum(source_rows, "code")

        def matrix(array, scatter):
            array = lax.psum_scatter(array, "dp", scatter_dimension=0, tiled=True)
            return lax.psum_scatter(array, "code", scatter_dimension=scatter, tiled=True).astype(F32)

        conv_flat = jnp.stack(
            [
                grads_first[0].reshape(9, channels, channels),
                grads_second[0][: 9 * channels].reshape(9, channels, channels),
            ]
        ).transpose(2, 0, 1, 3)
        conv_part = matrix(conv_flat, 3)
        down_flat = grads_second[0][9 * channels : 13 * channels]
        down_part = matrix(down_flat.reshape(4, channels, channels).transpose(1, 0, 2), 2)
        proj_part = matrix(grads_second[0][13 * channels :, :width], 1)
        norm_grad = lax.psum(norm_grad, ("dp", "code"))
        input_back = lax.all_to_all(
            image_parts[0][None], "dp", split_axis=2, concat_axis=1, tiled=True
        ).astype(F32)

    pixels_all = crop_dev * pixels * dp_count * code_count
    weight_rate = WEIGHT_RATE / math.sqrt(pixels_all)
    norm_rate = NORM_RATE / math.sqrt(pixels_all)
    crops_all = crop_dev * dp_count * code_count
    mean_count = DEPTH * lat * crops_all / codes_all
    code_rate = CODE_RATE / math.sqrt(mean_count)
    conv_out = nesterov_step(conv_master, conv_moment, conv_average, conv_part, weight_rate)
    down_out = nesterov_step(down_master, down_moment, down_average, down_part, weight_rate)
    proj_out = nesterov_step(proj_master, proj_moment, proj_average, proj_part, weight_rate)
    norm_out = nesterov_step(norm_master, norm_moment, norm_average, norm_grad.T, norm_rate)

    counts_all, slope_sum = sums[0], sums[1]
    share = mean_count / (mean_count + counts_all)
    code_load = counts_all / mean_count
    cols = width // dp_count
    own_codes = lax.dynamic_slice_in_dim(codebook, dp_at * cols, cols, 1).T.astype(F32)
    code_grad = code_grad - own_codes * slope_sum[None, :]
    code_moment_new = MOMENTUM * code_moment.T + code_grad
    stepped = code_master.T - code_rate * (code_grad + MOMENTUM * code_moment_new)
    select = (
        repl_code.reshape(-1)[:, None] - code_at * code_dev
        == jnp.arange(code_dev, dtype=jnp.int32)[None, :]
    )
    chosen = jnp.sum(select.astype(F32), axis=0)
    renewed = mm(source_rows, select.astype(BF))
    code_master_new = stepped + (chosen * share)[None, :] * (renewed - stepped)
    code_average_new = AVERAGE_DECAY * code_average.T + (1.0 - AVERAGE_DECAY) * code_master_new
    return (
        quantized.reshape(1, crop_dev, lat, width),
        input_back,
        *conv_out,
        *down_out,
        *proj_out,
        *norm_out,
        code_moment_new.T,
        code_master_new.T,
        code_average_new.T,
        code_load,
    )


def solution(mesh):
    in_specs = (
        P("code", None, "dp", None),
        P("code", "dp"),
        P("code", "dp", None, None),
        P(),
        P(),
        P(),
        P(),
        P("code", None),
        P("dp", None, None, "code"),
        P("dp", None, None, "code"),
        P("dp", None, None, "code"),
        P("dp", None, "code"),
        P("dp", None, "code"),
        P("dp", None, "code"),
        P("dp", "code"),
        P("dp", "code"),
        P("dp", "code"),
        P(),
        P(),
        P(),
        P("code", "dp"),
        P("code", "dp"),
        P("code", "dp"),
        P(),
        P(),
    )
    out_specs = (
        P("code", "dp", None, None),
        P("code", None, "dp", None),
        P("dp", None, None, "code"),
        P("dp", None, None, "code"),
        P("dp", None, None, "code"),
        P("dp", None, "code"),
        P("dp", None, "code"),
        P("dp", None, "code"),
        P("dp", "code"),
        P("dp", "code"),
        P("dp", "code"),
        P(),
        P(),
        P(),
        P("code", "dp"),
        P("code", "dp"),
        P("code", "dp"),
        P("code"),
    )
    return jax.shard_map(body, mesh=mesh, in_specs=in_specs, out_specs=out_specs, check_vma=False)
```

time: 1070 us -> 467 us (0.44)
  matrix products: 204 us -> 1.4 us
  waiting for transfers between devices: 384 us -> 197 us
  blocking collectives: 144 us -> 0 us
  other arithmetic: 149 us -> 18.3 us
  Pallas kernels: 0 us -> 125 us
  local copies, waits for them, and re-layouts: 146 us -> 34.8 us
  starting transfers between devices: 13 us -> 78.7 us
  between operations: 16.2 us -> 2.27 us
    dot_general x96 -> x2, matrix products: 204 us -> 1.4 us  [mm(): return lax.dot_general(a, b, dims, preferred_element_type=F32)]
    reduce_scatter x5 -> x0, waiting for transfers between devices: 201 us -> none  [the longest x1 70.8 us: body(): lax.psum_scatter(conv_flat.astype(jnp.bfloat16), 'dp', scatter_dimension=...]
    ppermute x0 -> x69, waiting for transfers between devices: none -> 197 us  [swap(): return lax.ppermute(array, axis, [(i, i ^ bit) for i in range(count)])]
    psum x4 -> x0, waiting for transfers between devices: 129 us -> none  [body(): lax.psum(grad_rows.reshape(rows_count, width).astype(jnp.bfloat16), 'code')]
    pallas_call x0 -> x5, Pallas kernels: none -> 125 us  [the longest x1 91.8 us: quant_call(): pl.pallas_call(functools.partial(quant_kernel, n_shard), out_shape=[jax.S...]
    psum x2 -> x0, blocking collectives: 83.1 us -> none  [the longest x1 44.4 us: body(): lax.psum(jnp.stack([gain_first, bias_first, gain_second, bias_second], ax...]
    ppermute x0 -> x69, starting transfers between devices: none -> 72.9 us  [swap(): return lax.ppermute(array, axis, [(i, i ^ bit) for i in range(count)])]
    all_gather x11 -> x0, blocking collectives: 60.9 us -> none  [the longest x8 41.9 us: combined_all(): lax.all_gather(part.astype(kind), axis)]
  transfers between devices with their start and end apart: 18 -> 70, of which waited for: 11 -> 42; matrix products, arithmetic and copies ran while one was open for 23% -> 8% of each run, Pallas kernels for 0% -> 7%
where the time goes in v1:
time: 467 us; the launch traced here: 458 us
  waiting for transfers between devices  197 us (42%)
  Pallas kernels  125 us (27%)
  starting transfers between devices  78.7 us (17%)
  local copies, waits for them, and re-layouts  34.8 us (7%)
  other arithmetic  18.3 us (4%)
    ppermute x69, waiting for transfers between devices, swap(): return lax.ppermute(array, axis, [(i, i ^ bit) for i in range(count)])  197 us
    pallas_call x1, Pallas kernels, quant_call(): pl.pallas_call(functools.partial(quant_kernel, n_shard), out_shape=[jax.S...  91.8 us
    ppermute x69, starting transfers between devices, swap(): return lax.ppermute(array, axis, [(i, i ^ bit) for i in range(count)])  72.9 us
    unnamed x91, local copies, waits for them, and re-layouts  23.7 us
    pallas_call x1, Pallas kernels, second_call(): pl.pallas_call(functools.partial(second_kernel, side, len(grads), n_in, n...  12.5 us
    pallas_call x1, Pallas kernels, forward_call(): pl.pallas_call(functools.partial(forward_kernel, side), out_shape=[jax.Sh...  9.64 us
  transfers between devices with their start and end apart: 70, of which 42 were waited for; matrix products, arithmetic and copies ran while one was open for 8% of the time, Pallas kernels for 7%

profile of v1, /device:TPU:0, one launch (start us, length us, event | category | flops | bytes accessed | tf_op | source)
XLA Modules:
  0.0 457.6 jit_solution(8725528731178649653)
XLA Ops:
  7.9 5.8 %all-to-all-start = ((bf16[1,16,32,512]{3,2,0,1:T(8,128)(2,1)}), bf16[1,16,32,512]{3,2,0,1:T(8,128)(2,1)S(1)}, u32[]{:S(2)}, u32[]{:S(2)}) async-start(bf16[1,16,32,512]{3,2,0,1:T(8,128)(2,1)} %bitcast.2), calls=%async_computation | async-start | bytes 1048576 | tf_op jit(solution)/shard_map/all_to_all | solution.py:787
  18.3 9.3 %copy.245 = bf16[512,2,9,512]{3,0,2,1:T(8,128)(2,1)} copy(bf16[512,2,9,512]{3,1,2,0:T(2,128)(2,1)} %param.28) | data formatting | bytes 18874368 | tf_op args[3]
  32.6 66.4 %collective-permute-done.2 = f32[4096]{0:T(1024)S(1)} collective-permute-done((f32[4096]{0:T(1024)S(1)}, f32[4096]{0:T(1024)S(1)}, u32[]{:S(2)}, u32[]{:S(2)}) %collective-permute-start.2) | collective-permute-done | bytes 16416 | tf_op jit(solution)/shard_map/ppermute | solution.py:716
  101.5 9.6 %residual_forward.1 = (f32[2,256,512]{2,1,0:T(8,128)S(1)}, f32[2,8,512]{2,1,0:T(8,128)S(1)}, bf16[4,128,512]{2,1,0:T(8,128)(2,1)S(1)}, bf16[128,512]{1,0:T(8,128)(2,1)S(1)}, bf16[128,256]{1,0:T(8,128)(2,1)S(1)}) custom-call(bf16[2,256,512]{2,1,0:T(8,128)(2,1)S(1)} %bitcast.415, f32[4,512]{1,0:T(4,128)S(1)} %convert_bitcast_fusion.norm_ref, ...), custom_call_target="tpu_custom_call" | custom-call | flops 9663676416 | bytes 16777216 | tf_op jit(solution)/shard_map/residual_forward/pallas_call | solution.py:195
  113.6 91.8 %soft_quantize.1 = (f32[128,256]{1,0:T(8,128)}, bf16[128,256]{1,0:T(8,128)(2,1)}, bf16[4,128,256]{2,1,0:T(8,128)(2,1)}, f32[2,16384]{1,0:T(2,128)}, bf16[4,8,32,4096]{3,2,1,0:T(8,128)(2,1)}) custom-call(s32[2]{0:T(128)} %pad_add_fusion.place_ref, bf16[128,256]{1,0:T(8,128)(2,1)} %copy-done.9, f32[1,16384]{1,0:T(1,128)} %bitcast.455, ...), custom_call_target="tpu_custom_call" | custom-call | flops 25769803776 | bytes 18874368 | tf_op jit(solution)/shard_map/soft_quantize/pallas_call | solution.py:363
  205.5 4.8 %slice_bitcast_fusion.1 = (bf16[8,32,4096]{2,1,0:T(8,128)(2,1)}, bf16[8,32,4096]{2,1,0:T(8,128)(2,1)}) fusion(bf16[4,8,32,4096]{3,2,1,0:T(8,128)(2,1)} %get-tuple-element.67), kind=kLoop, calls=%fused_computation.16 | loop fusion | bytes 8388608 | tf_op jit(solution)/shard_map/squeeze | solution.py:861
  213.4 12.5 %second_backward.1 = (bf16[2,8,864,128]{3,2,1,0:T(8,128)(2,1)S(1)}, bf16[2,8,864,128]{3,2,1,0:T(8,128)(2,1)}, bf16[2,256,512]{2,1,0:T(8,128)(2,1)S(1)}, bf16[2,256,512]{2,1,0:T(8,128)(2,1)S(1)}, f32[8,512]{1,0:T(8,128)S(1)}) custom-call(s32[2]{0:T(128)S(1)} %copy-done.2, bf16[128,256]{1,0:T(8,128)(2,1)S(1)} %copy-done.8, ...), custom_call_target="tpu_custom_call" | custom-call | flops 4831838208 | bytes 12582912 | tf_op jit(solution)/shard_map/second_backward/pallas_call | solution.py:655
  226.0 6.5 %first_image_backward.1 = (bf16[2,32,512]{2,1,0:T(8,128)(2,1)S(1)}, bf16[2,32,512]{2,1,0:T(8,128)(2,1)S(1)}, bf16[2,32,512]{2,1,0:T(8,128)(2,1)S(1)}, bf16[2,32,...) custom-call(s32[2]{0:T(128)S(1)} %copy-done.2, ...), custom_call_target="tpu_custom_call" | custom-call | flops 2415919104 | bytes 12582912 | tf_op jit(solution)/shard_map/first_image_backward/pallas_call | solution.py:695
  234.4 4.1 first_weight_backward.1
  256.1 3.3 collective-permute-done.6
  260.9 3.3 collective-permute-done.7
  266.1 3.8 collective-permute-done.8
  275.2 4.5 collective-permute-start.11
  280.0 4.4 collective-permute-done.65
  290.1 5.1 %collective-permute-done.12 = bf16[2,32,512]{2,1,0:T(8,128)(2,1)S(1)} collective-permute-done((bf16[2,32,512]{2,1,0:T(8,128)(2,1)S(1)}, bf16[2,32,512]{2,1,0:T(8,128)(2,1)S(1)}, u32[]{:S(2)}, u32[]{:S(2)}) %collective-permute-start.12) | collective-permute-done | bytes 65568 | tf_op jit(solution)/shard_map/ppermute | solution.py:716
  296.4 4.8 %collective-permute-done.63 = f32[2,4096]{1,0:T(2,128)S(1)} collective-permute-done((f32[2,4096]{1,0:T(2,128)S(1)}, f32[2,4096]{1,0:T(2,128)S(1)}, u32[]{:S(2)}, u32[]{:S(2)}) %collective-permute-start.63) | collective-permute-done | bytes 32800 | tf_op jit(solution)/shard_map/ppermute | solution.py:716
  303.0 4.3 fusion.3
  311.3 13.8 %collective-permute-done.54 = bf16[2,2,2,32,1280]{4,3,1,2,0:T(8,128)(2,1)S(1)} collective-permute-done((bf16[2,2,2,32,1280]{4,3,1,2,0:T(8,128)(2,1)S(1)}, bf16[2,2,2,32,1280]{4,3,1,2,0:T(8,128)(2,1)S(1)}, u32[]{:S(2)}, u32[]{:S(2)}) %collective-permute-start.54) | collective-permute-done | bytes 655392 | tf_op jit(solution)/shard_map/ppermute | solution.py:716
  325.5 7.9 %collective-permute-done.14 = bf16[2,2,2,192,128]{4,3,0,1,2:T(8,128)(2,1)S(1)} collective-permute-done((bf16[2,2,2,192,128]{4,3,0,1,2:T(8,128)(2,1)S(1)}, bf16[2,2,2,192,128]{4,3,0,1,2:T(8,128)(2,1)S(1)}, u32[]{:S(2)}, u32[]{:S(2)}) %collective-permute-start.14) | collective-permute-done | bytes 393248 | tf_op jit(solution)/shard_map/ppermute | solution.py:716
  336.2 6.6 %collective-permute-done.22 = bf16[2,2,2,192,128]{4,3,1,2,0:T(8,128)(2,1)S(1)} collective-permute-done((bf16[2,2,2,192,128]{4,3,1,2,0:T(8,128)(2,1)S(1)}, bf16[2,2,2,192,128]{4,3,1,2,0:T(8,128)(2,1)S(1)}, u32[]{:S(2)}, u32[]{:S(2)}) %collective-permute-start.22) | collective-permute-done | bytes 393248 | tf_op jit(solution)/shard_map/ppermute | solution.py:716
  346.7 5.3 %collective-permute-done.50 = bf16[2,2,2,32,1408]{4,3,1,0,2:T(8,128)(2,1)S(1)} collective-permute-done((bf16[2,2,2,32,1408]{4,3,1,0,2:T(8,128)(2,1)S(1)}, bf16[2,2,2,32,1408]{4,3,1,0,2:T(8,128)(2,1)S(1)}, u32[]{:S(2)}, u32[]{:S(2)}) %collective-permute-start.50) | collective-permute-done | bytes 720928 | tf_op jit(solution)/shard_map/ppermute | solution.py:716
  360.3 4.0 collective-permute-done.16
  365.9 3.1 collective-permute-done.20
  369.3 4.3 collective-permute-done.24
  375.9 4.2 collective-permute-done.17
  380.1 3.4 collective-permute-start.21
  385.6 3.4 collective-permute-start.25
  389.0 3.8 collective-permute-done.25
  394.5 3.6 collective-permute-done.56
  400.3 3.3 collective-permute-done.57
  419.4 10.0 %collective-permute-done.27 = bf16[2,2,2,288,128]{4,3,0,1,2:T(8,128)(2,1)S(1)} collective-permute-done((bf16[2,2,2,288,128]{4,3,0,1,2:T(8,128)(2,1)S(1)}, bf16[2,2,2,288,128]{4,3,0,1,2:T(8,128)(2,1)S(1)}, u32[]{:S(2)}, u32[]{:S(2)}) %collective-permute-start.27) | collective-permute-done | bytes 589856 | tf_op jit(solution)/shard_map/ppermute | solution.py:716
  432.3 4.1 collective-permute-done.28
  (347 shorter events, 130.4 us)
Async XLA Ops:
  2.9 14.3 %collective-permute-start = (f32[4096]{0:T(1024)S(1)}, f32[4096]{0:T(1024)S(1)}, u32[]{:S(2)}, u32[]{:S(2)}) collective-permute-start(f32[4096]{0:T(1024)S(1)} %broadcast_multiply_fusion), channel_id=1, source_target_pairs={{0,1},{1,0},{2,3},{3,2},{4,5},{5,4},{6,7},{7,6},{8,9},{9,8},{10,11... | collective-permute-start | bytes 49160 | tf_op jit(solution)/shard_map/ppermute | solution.py:716
  3.5 29.2 %collective-permute-start.1 = (f32[4096]{0:T(1024)S(1)}, f32[4096]{0:T(1024)S(1)}, u32[]{:S(2)}, u32[]{:S(2)}) collective-permute-start(f32[4096]{0:T(1024)S(1)} %broadcast_multiply_fusion), channel_id=1, source_target_pairs={{0,2},{1,3},{2,0},{3,1},{4,6},{5,7},{6,4},{7,5},{8,10},{9,11},{10,... | collective-permute-start | bytes 49160 | tf_op jit(solution)/shard_map/ppermute | solution.py:716
  6.0 107.6 %collective-permute-start.3 = (bf16[4096,256]{1,0:T(8,128)(2,1)}, bf16[4096,256]{1,0:T(8,128)(2,1)}, u32[]{:S(2)}, u32[]{:S(2)}) collective-permute-start(bf16[4096,256]{1,0:T(8,128)(2,1)} %rest_0_.1), channel_id=1, source_target_pairs={{0,1},{1,0},{2,3},{3,2},{4,5},{5,4},{6,7},{7,6},{8,9},{9,8},{10,11... | collective-permute-start | bytes 6291464 | tf_op jit(solution)/shard_map/ppermute | solution.py:716
  6.2 107.4 %collective-permute-start.4 = (bf16[4096,256]{1,0:T(8,128)(2,1)}, bf16[4096,256]{1,0:T(8,128)(2,1)}, u32[]{:S(2)}, u32[]{:S(2)}) collective-permute-start(bf16[4096,256]{1,0:T(8,128)(2,1)} %rest_0_.1), channel_id=1, source_target_pairs={{0,2},{1,3},{2,0},{3,1},{4,6},{5,7},{6,4},{7,5},{8,10},{9,11},{10,... | collective-permute-start | bytes 6291464 | tf_op jit(solution)/shard_map/ppermute | solution.py:716
  6.5 107.1 %collective-permute-start.5 = (bf16[4096,256]{1,0:T(8,128)(2,1)}, bf16[4096,256]{1,0:T(8,128)(2,1)}, u32[]{:S(2)}, u32[]{:S(2)}) collective-permute-start(bf16[4096,256]{1,0:T(8,128)(2,1)} %rest_0_.1), channel_id=1, source_target_pairs={{0,3},{1,2},{2,1},{3,0},{4,7},{5,6},{6,5},{7,4},{8,11},{9,10},{10,... | collective-permute-start | bytes 6291464 | tf_op jit(solution)/shard_map/ppermute | solution.py:716
  7.9 91.7 %all-to-all-start = ((bf16[1,16,32,512]{3,2,0,1:T(8,128)(2,1)}), bf16[1,16,32,512]{3,2,0,1:T(8,128)(2,1)S(1)}, u32[]{:S(2)}, u32[]{:S(2)}) async-start(bf16[1,16,32,512]{3,2,0,1:T(8,128)(2,1)} %bitcast.2), calls=%async_computation | async-start | bytes 1048576 | tf_op jit(solution)/shard_map/all_to_all | solution.py:787
  17.3 81.7 %collective-permute-start.2 = (f32[4096]{0:T(1024)S(1)}, f32[4096]{0:T(1024)S(1)}, u32[]{:S(2)}, u32[]{:S(2)}) collective-permute-start(f32[4096]{0:T(1024)S(1)} %broadcast_multiply_fusion), channel_id=1, source_target_pairs={{0,3},{1,2},{2,1},{3,0},{4,7},{5,6},{6,5},{7,4},{8,11},{9,10},{10,... | collective-permute-start | bytes 49160 | tf_op jit(solution)/shard_map/ppermute | solution.py:716
  210.3 92.7 %collective-permute-start.44 = (bf16[8,32,4096]{2,1,0:T(8,128)(2,1)}, bf16[8,32,4096]{2,1,0:T(8,128)(2,1)}, u32[]{:S(2)}, u32[]{:S(2)}) collective-permute-start(bf16[8,32,4096]{2,1,0:T(8,128)(2,1)} %get-tuple-element.137), channel_id=1, source_target_pairs={{0,1},{1,0},{2,3},{3,2},{4,5},{5,4},{6,7},{7,6},{8,9},{9,8},{10,11... | collective-permute-start | bytes 6291464 | tf_op jit(solution)/shard_map/ppermute | solution.py:716
  210.9 35.6 %collective-permute-start.59 = (f32[2,4096]{1,0:T(2,128)S(1)}, f32[2,4096]{1,0:T(2,128)S(1)}, u32[]{:S(2)}, u32[]{:S(2)}) collective-permute-start(f32[2,4096]{1,0:T(2,128)S(1)} %bitcast.457), channel_id=1, source_target_pairs={{0,1},{1,0},{2,3},{3,2},{4,5},{5,4},{6,7},{7,6},{8,9},{9,8},{10,11... | collective-permute-start | bytes 98312 | tf_op jit(solution)/shard_map/ppermute | solution.py:716
  240.2 31.3 %collective-permute-start.64 = (bf16[2,2,32,256]{3,2,1,0:T(8,128)(2,1)S(1)}, bf16[2,2,32,256]{3,2,1,0:T(8,128)(2,1)S(1)}, u32[]{:S(2)}, u32[]{:S(2)}) collective-permute-start(bf16[2,2,32,256]{3,2,1,0:T(8,128)(2,1)S(1)} %dynamic-slice_bitcast_fusion), channel_id=1, source_target_pairs={{0,16},{4,20},{8,24},{12,28},{16,0},{20,4},{24,8},{28,12},{1,17},{... | collective-permute-start | bytes 196616 | tf_op jit(solution)/shard_map/ppermute | solution.py:716
  242.8 60.2 %collective-permute-start.45 = (bf16[8,32,4096]{2,1,0:T(8,128)(2,1)S(1)}, bf16[8,32,4096]{2,1,0:T(8,128)(2,1)S(1)}, u32[]{:S(2)}, u32[]{:S(2)}) collective-permute-start(bf16[8,32,4096]{2,1,0:T(8,128)(2,1)S(1)} %copy-done.11), channel_id=1, source_target_pairs={{0,1},{1,0},{2,3},{3,2},{4,5},{5,4},{6,7},{7,6},{8,9},{9,8},{10,11... | collective-permute-start | bytes 6291464 | tf_op jit(solution)/shard_map/ppermute | solution.py:716
  253.3 160.7 %collective-permute-start.26 = (bf16[2,8,864,128]{3,2,1,0:T(8,128)(2,1)}, bf16[2,8,864,128]{3,2,1,0:T(8,128)(2,1)S(1)}, u32[]{:S(2)}, u32[]{:S(2)}) collective-permute-start(bf16[2,8,864,128]{3,2,1,0:T(8,128)(2,1)} %get-tuple-element.64), channel_id=1, source_target_pairs={{0,1},{1,0},{2,3},{3,2},{4,5},{5,4},{6,7},{7,6},{8,9},{9,8},{10,11... | collective-permute-start | bytes 10616840 | tf_op jit(solution)/shard_map/ppermute | solution.py:716
  271.5 8.2 %collective-permute-start.10 = (bf16[2,32,512]{2,1,0:T(8,128)(2,1)S(1)}, bf16[2,32,512]{2,1,0:T(8,128)(2,1)S(1)}, u32[]{:S(2)}, u32[]{:S(2)}) collective-permute-start(bf16[2,32,512]{2,1,0:T(8,128)(2,1)S(1)} %get-tuple-element.58), channel_id=1, source_target_pairs={{0,20},{4,16},{8,28},{12,24},{16,4},{20,0},{24,12},{28,8},{1,21},{... | collective-permute-start | bytes 196616 | tf_op jit(solution)/shard_map/ppermute | solution.py:716
  275.2 10.1 %collective-permute-start.11 = (bf16[2,32,512]{2,1,0:T(8,128)(2,1)S(1)}, bf16[2,32,512]{2,1,0:T(8,128)(2,1)S(1)}, u32[]{:S(2)}, u32[]{:S(2)}) collective-permute-start(bf16[2,32,512]{2,1,0:T(8,128)(2,1)S(1)} %get-tuple-element.59), channel_id=1, source_target_pairs={{0,24},{4,28},{8,16},{12,20},{16,8},{20,12},{24,0},{28,4},{1,25},{... | collective-permute-start | bytes 196616 | tf_op jit(solution)/shard_map/ppermute | solution.py:716
  295.2 14.0 %collective-permute-start.13 = (bf16[2,8,576,128]{3,2,1,0:T(8,128)(2,1)S(1)}, bf16[2,8,576,128]{3,2,1,0:T(8,128)(2,1)S(1)}, u32[]{:S(2)}, u32[]{:S(2)}) collective-permute-start(bf16[2,8,576,128]{3,2,1,0:T(8,128)(2,1)S(1)} %get-tuple-element.62), channel_id=1, source_target_pairs={{0,1},{1,0},{2,3},{3,2},{4,5},{5,4},{6,7},{7,6},{8,9},{9,8},{10,11... | collective-permute-start | bytes 7077896 | tf_op jit(solution)/shard_map/ppermute | solution.py:716
  301.2 110.7 %collective-permute-start.68 = (bf16[32,256]{1,0:T(8,128)(2,1)S(1)}, bf16[32,256]{1,0:T(8,128)(2,1)S(1)}, u32[]{:S(2)}, u32[]{:S(2)}) collective-permute-start(bf16[32,256]{1,0:T(8,128)(2,1)S(1)} %add_convert_fusion.3), channel_id=1, source_target_pairs={{0,2},{1,3},{2,0},{3,1},{4,6},{5,7},{6,4},{7,5},{8,10},{9,11},{10,... | collective-permute-start | bytes 49160 | tf_op jit(solution)/shard_map/ppermute | solution.py:716
  307.7 36.9 %collective-permute-start.46 = (bf16[2,2,2,32,1408]{4,3,0,1,2:T(8,128)(2,1)S(1)}, bf16[2,2,2,32,1408]{4,3,0,1,2:T(8,128)(2,1)S(1)}, u32[]{:S(2)}, u32[]{:S(2)}) collective-permute-start(bf16[2,2,2,32,1408]{4,3,0,1,2:T(8,128)(2,1)S(1)} %copy.159), channel_id=1, source_target_pairs={{0,2},{1,3},{2,0},{3,1},{4,6},{5,7},{6,4},{7,5},{8,10},{9,11},{10,... | collective-permute-start | bytes 2162696 | tf_op jit(solution)/shard_map/ppermute | solution.py:716
  309.1 15.9 %collective-permute-start.54 = (bf16[2,2,2,32,1280]{4,3,1,2,0:T(8,128)(2,1)S(1)}, bf16[2,2,2,32,1280]{4,3,1,2,0:T(8,128)(2,1)S(1)}, u32[]{:S(2)}, u32[]{:S(2)}) collective-permute-start(bf16[2,2,2,32,1280]{4,3,1,2,0:T(8,128)(2,1)S(1)} %bitcast.439), channel_id=1, source_target_pairs={{0,8},{4,12},{8,0},{12,4},{16,24},{20,28},{24,16},{28,20},{1,9},{5... | collective-permute-start | bytes 1966088 | tf_op jit(solution)/shard_map/ppermute | solution.py:716
  310.0 23.4 %collective-permute-start.14 = (bf16[2,2,2,192,128]{4,3,0,1,2:T(8,128)(2,1)S(1)}, bf16[2,2,2,192,128]{4,3,0,1,2:T(8,128)(2,1)S(1)}, u32[]{:S(2)}, u32[]{:S(2)}) collective-permute-start(bf16[2,2,2,192,128]{4,3,0,1,2:T(8,128)(2,1)S(1)} %bitcast.450), channel_id=1, source_target_pairs={{0,2},{1,3},{2,0},{3,1},{4,6},{5,7},{6,4},{7,5},{8,10},{9,11},{10,... | collective-permute-start | bytes 1179656 | tf_op jit(solution)/shard_map/ppermute | solution.py:716
  325.1 9.5 %collective-permute-start.18 = (bf16[2,2,2,192,128]{4,3,1,0,2:T(8,128)(2,1)S(1)}, bf16[2,2,2,192,128]{4,3,1,0,2:T(8,128)(2,1)S(1)}, u32[]{:S(2)}, u32[]{:S(2)}) collective-permute-start(bf16[2,2,2,192,128]{4,3,1,0,2:T(8,128)(2,1)S(1)} %bitcast.449), channel_id=1, source_target_pairs={{0,4},{4,0},{8,12},{12,8},{16,20},{20,16},{24,28},{28,24},{1,5},{5... | collective-permute-start | bytes 1179656 | tf_op jit(solution)/shard_map/ppermute | solution.py:716
  333.4 18.6 %collective-permute-start.50 = (bf16[2,2,2,32,1408]{4,3,1,0,2:T(8,128)(2,1)S(1)}, bf16[2,2,2,32,1408]{4,3,1,0,2:T(8,128)(2,1)S(1)}, u32[]{:S(2)}, u32[]{:S(2)}) collective-permute-start(bf16[2,2,2,32,1408]{4,3,1,0,2:T(8,128)(2,1)S(1)} %bitcast.438), channel_id=1, source_target_pairs={{0,4},{4,0},{8,12},{12,8},{16,20},{20,16},{24,28},{28,24},{1,5},{5... | collective-permute-start | bytes 2162696 | tf_op jit(solution)/shard_map/ppermute | solution.py:716
  334.6 8.2 %collective-permute-start.22 = (bf16[2,2,2,192,128]{4,3,1,2,0:T(8,128)(2,1)S(1)}, bf16[2,2,2,192,128]{4,3,1,2,0:T(8,128)(2,1)S(1)}, u32[]{:S(2)}, u32[]{:S(2)}) collective-permute-start(bf16[2,2,2,192,128]{4,3,1,2,0:T(8,128)(2,1)S(1)} %bitcast.448), channel_id=1, source_target_pairs={{0,8},{4,12},{8,0},{12,4},{16,24},{20,28},{24,16},{28,20},{1,9},{5... | collective-permute-start | bytes 1179656 | tf_op jit(solution)/shard_map/ppermute | solution.py:716
  342.8 31.4 %collective-permute-start.55 = (bf16[2,2,32,1280]{3,2,0,1:T(8,128)(2,1)S(1)}, bf16[2,2,32,1280]{3,2,0,1:T(8,128)(2,1)S(1)}, u32[]{:S(2)}, u32[]{:S(2)}) collective-permute-start(bf16[2,2,32,1280]{3,2,0,1:T(8,128)(2,1)S(1)} %slice_bitcast_fusion.6), channel_id=1, source_target_pairs={{0,2},{1,3},{2,0},{3,1},{4,6},{5,7},{6,4},{7,5},{8,10},{9,11},{10,... | collective-permute-start | bytes 983048 | tf_op jit(solution)/shard_map/ppermute | solution.py:716
  344.7 9.4 %collective-permute-start.15 = (bf16[2,2,192,128]{3,2,0,1:T(8,128)(2,1)S(1)}, bf16[2,2,192,128]{3,2,0,1:T(8,128)(2,1)S(1)}, u32[]{:S(2)}, u32[]{:S(2)}) collective-permute-start(bf16[2,2,192,128]{3,2,0,1:T(8,128)(2,1)S(1)} %slice_bitcast_fusion.18), channel_id=1, source_target_pairs={{0,4},{4,0},{8,12},{12,8},{16,20},{20,16},{24,28},{28,24},{1,5},{5... | collective-permute-start | bytes 589832 | tf_op jit(solution)/shard_map/ppermute | solution.py:716
  357.6 35.2 %collective-permute-start.47 = (bf16[2,2,32,1408]{3,2,0,1:T(8,128)(2,1)S(1)}, bf16[2,2,32,1408]{3,2,0,1:T(8,128)(2,1)S(1)}, u32[]{:S(2)}, u32[]{:S(2)}) collective-permute-start(bf16[2,2,32,1408]{3,2,0,1:T(8,128)(2,1)S(1)} %slice_bitcast_fusion.4), channel_id=1, source_target_pairs={{0,4},{4,0},{8,12},{12,8},{16,20},{20,16},{24,28},{28,24},{1,5},{5... | collective-permute-start | bytes 1081352 | tf_op jit(solution)/shard_map/ppermute | solution.py:716
  373.6 20.8 %collective-permute-start.51 = (bf16[2,2,32,1408]{3,2,1,0:T(8,128)(2,1)S(1)}, bf16[2,2,32,1408]{3,2,1,0:T(8,128)(2,1)S(1)}, u32[]{:S(2)}, u32[]{:S(2)}) collective-permute-start(bf16[2,2,32,1408]{3,2,1,0:T(8,128)(2,1)S(1)} %slice_bitcast_fusion.2), channel_id=1, source_target_pairs={{0,8},{4,12},{8,0},{12,4},{16,24},{20,28},{24,16},{28,20},{1,9},{5... | collective-permute-start | bytes 1081352 | tf_op jit(solution)/shard_map/ppermute | solution.py:716
  385.6 7.2 %collective-permute-start.25 = (bf16[192,128]{1,0:T(8,128)(2,1)S(1)}, bf16[192,128]{1,0:T(8,128)(2,1)S(1)}, u32[]{:S(2)}, u32[]{:S(2)}) collective-permute-start(bf16[192,128]{1,0:T(8,128)(2,1)S(1)} %slice_bitcast_fusion.50), channel_id=1, source_target_pairs={{0,16},{4,20},{8,24},{12,28},{16,0},{20,4},{24,8},{28,12},{1,17},{... | collective-permute-start | bytes 147464 | tf_op jit(solution)/shard_map/ppermute | solution.py:716
  393.0 10.6 %collective-permute-start.48 = (bf16[2,32,1408]{2,1,0:T(8,128)(2,1)S(1)}, bf16[2,32,1408]{2,1,0:T(8,128)(2,1)S(1)}, u32[]{:S(2)}, u32[]{:S(2)}) collective-permute-start(bf16[2,32,1408]{2,1,0:T(8,128)(2,1)S(1)} %slice_bitcast_fusion.22), channel_id=1, source_target_pairs={{0,8},{4,12},{8,0},{12,4},{16,24},{20,28},{24,16},{28,20},{1,9},{5... | collective-permute-start | bytes 540680 | tf_op jit(solution)/shard_map/ppermute | solution.py:716
  415.0 14.3 %collective-permute-start.27 = (bf16[2,2,2,288,128]{4,3,0,1,2:T(8,128)(2,1)S(1)}, bf16[2,2,2,288,128]{4,3,0,1,2:T(8,128)(2,1)S(1)}, u32[]{:S(2)}, u32[]{:S(2)}) collective-permute-start(bf16[2,2,2,288,128]{4,3,0,1,2:T(8,128)(2,1)S(1)} %bitcast.442), channel_id=1, source_target_pairs={{0,2},{1,3},{2,0},{3,1},{4,6},{5,7},{6,4},{7,5},{8,10},{9,11},{10,... | collective-permute-start | bytes 1769480 | tf_op jit(solution)/shard_map/ppermute | solution.py:716
  416.6 13.6 %collective-permute-start.31 = (bf16[2,2,2,288,128]{4,3,1,0,2:T(8,128)(2,1)S(1)}, bf16[2,2,2,288,128]{4,3,1,0,2:T(8,128)(2,1)S(1)}, u32[]{:S(2)}, u32[]{:S(2)}) collective-permute-start(bf16[2,2,2,288,128]{4,3,1,0,2:T(8,128)(2,1)S(1)} %bitcast.443), channel_id=1, source_target_pairs={{0,4},{4,0},{8,12},{12,8},{16,20},{20,16},{24,28},{28,24},{1,5},{5... | collective-permute-start | bytes 1769480 | tf_op jit(solution)/shard_map/ppermute | solution.py:716
  417.1 14.4 %collective-permute-start.35 = (bf16[2,2,2,288,128]{4,3,1,2,0:T(8,128)(2,1)S(1)}, bf16[2,2,2,288,128]{4,3,1,2,0:T(8,128)(2,1)S(1)}, u32[]{:S(2)}, u32[]{:S(2)}) collective-permute-start(bf16[2,2,2,288,128]{4,3,1,2,0:T(8,128)(2,1)S(1)} %bitcast.441), channel_id=1, source_target_pairs={{0,8},{4,12},{8,0},{12,4},{16,24},{20,28},{24,16},{28,20},{1,9},{5... | collective-permute-start | bytes 1769480 | tf_op jit(solution)/shard_map/ppermute | solution.py:716
  430.4 7.3 %collective-permute-start.32 = (bf16[2,2,288,128]{3,2,1,0:T(8,128)(2,1)S(1)}, bf16[2,2,288,128]{3,2,1,0:T(8,128)(2,1)S(1)}, u32[]{:S(2)}, u32[]{:S(2)}) collective-permute-start(bf16[2,2,288,128]{3,2,1,0:T(8,128)(2,1)S(1)} %slice_bitcast_fusion.10), channel_id=1, source_target_pairs={{0,8},{4,12},{8,0},{12,4},{16,24},{20,28},{24,16},{28,20},{1,9},{5... | collective-permute-start | bytes 884744 | tf_op jit(solution)/shard_map/ppermute | solution.py:716
  (77 other events, 662.6 us)
